TPU v7x, 32 devices: a whole 2x2x4 slice. The times are simulated.
32 devices in a mesh: inner: 4 (over y, x), outer: 8 (over z, core).
Axes of the slice: x: 2, y: 2, z: 4, core: 2. Of those that a mesh axis runs over, the one named last changes fastest.
Arguments:
- queries: bfloat16 [8, 2048, 768], P('outer', 'inner'), may hold values from -8 to 8
- key_rows: bfloat16 [8, 2048, 768], P('outer', 'inner'), may hold values from -8 to 8
- values: bfloat16 [8, 2048, 768], P('outer', 'inner'), may hold values from -6 to 6
- out_weight: bfloat16 [768, 768], replicated, may hold values from -0.21875 to 0.21875
Outputs:
- attention_out: bfloat16 [8, 2048, 768], P('outer', 'inner')
All inputs are finite; a program needn't handle non-finite values.
Results may differ from a plain program's by a relative error of at most 0.0052.
Values may be sent and summed in bfloat16 or wider, within the bound.
No kernel may reach another device: no remote copies, remote signals or barrier semaphores. Data moves between devices by JAX's collectives and lax.ppermute only.
A program may use at most 64 MiB of HBM per device.

v0:
```python
import jax
import jax.numpy as jnp
from jax import lax
from jax.sharding import PartitionSpec as P

HEADS = 12
HEAD_DIM = 64
GSTEP = 64


def partner_2(block, axis, distance):
    count = lax.axis_size(axis)
    route = []
    for low in range(count):
        high = low | 1 << distance
        if high != low and high < count:
            route += [(low, high), (high, low)]
    return lax.ppermute(block, axis, route)


def head_terms(query_part, level_set, scale_factor):
    scores = (
        jnp.einsum("td,nd->tn", query_part, level_set[0], preferred_element_type=jnp.float32)
        * scale_factor
    )
    row_peak = jnp.max(scores, axis=1, keepdims=True)
    expo_rows = jnp.exp(scores - row_peak)
    row_total = jnp.sum(expo_rows, axis=1, keepdims=True)
    weights = expo_rows.astype(jnp.bfloat16)
    numerator = jnp.dot(weights, level_set[1], preferred_element_type=jnp.float32)
    return (row_peak, row_total, numerator)


def merge_levels(all_terms):
    overall_peak = jnp.max(jnp.stack([entry[0] for entry in all_terms]), axis=0)
    numer_sum = jnp.zeros_like(all_terms[0][2])
    denom_sum = jnp.zeros_like(all_terms[0][1])
    for entry in all_terms:
        factor = jnp.exp(entry[0] - overall_peak)
        numer_sum = numer_sum + factor * entry[2]
        denom_sum = denom_sum + factor * entry[1]
    return numer_sum / denom_sum


def local(queries, key_rows, values, out_weight):
    query_rows = queries[0]
    kv_pair = jnp.stack([key_rows[0], values[0]])
    inner_bits = lax.axis_size("inner").bit_length() - 1
    level_sets = [kv_pair]
    current = kv_pair
    for level_bit in range(inner_bits):
        kv_half = current[:, ::2]
        partner = partner_2(kv_half, "inner", level_bit)
        current = jnp.concatenate([kv_half, partner], axis=1)
        level_sets.append(current)
    top_half = level_sets[-1][:, ::2]
    outer_partner = partner_2(top_half, "outer", 0)
    level_sets.append(jnp.concatenate([top_half, outer_partner], axis=1))
    own_rows = kv_pair[:, ::GSTEP]
    inner_set = lax.all_gather(own_rows, "inner", axis=1, tiled=True)
    global_set = lax.all_gather(inner_set, "outer", axis=1, tiled=True)
    level_sets.append(global_set)
    scale_factor = HEAD_DIM ** (-0.5)

    def per_head(head_index):
        col_start = head_index * HEAD_DIM
        head_query = lax.dynamic_slice_in_dim(query_rows, col_start, HEAD_DIM, 1)
        collected = [
            head_terms(
                head_query,
                lax.dynamic_slice_in_dim(level_set, col_start, HEAD_DIM, 2),
                scale_factor,
            )
            for level_set in level_sets
        ]
        return merge_levels(collected)

    merged = lax.map(per_head, jnp.arange(HEADS, dtype=jnp.int32))
    token_count = query_rows.shape[0]
    attended = merged.transpose(1, 0, 2).reshape(token_count, HEADS * HEAD_DIM).astype(jnp.bfloat16)
    result = jnp.dot(attended, out_weight, preferred_element_type=jnp.float32).astype(jnp.bfloat16)
    return result[None]


def solution(mesh):
    placed = (P("outer", "inner", None), P("outer", "inner", None), P("outer", "inner", None), P())
    return jax.shard_map(
        local, mesh=mesh, in_specs=placed, out_specs=P("outer", "inner", None), check_vma=False
    )
```

profile of v0, /device:TPU:0, one launch (start us, length us, event | category | flops | bytes accessed | tf_op | source)
XLA Modules:
  0.0 305.6 jit_solution(9134958266598548399)
XLA Ops:
  0.0 2.2 constant_dynamic-update-slice_fusion.1
  3.2 6.9 %slice.42 = bf16[2,256,768]{2,1,0:T(8,128)(2,1)S(1)} slice(bf16[2,512,768]{2,1,0:T(8,128)(2,1)} %constant_dynamic-update-slice_fusion), slice={[0:2:1], [0:512:2], [0:768:1]} | slice | bytes 1572864 | tf_op jit(solution)/shard_map/slice | solution.py:52
  10.1 3.0 collective-permute-start
  13.2 17.5 %collective-permute-done = bf16[2,256,768]{2,1,0:T(8,128)(2,1)S(1)} collective-permute-done((bf16[2,256,768]{2,1,0:T(8,128)(2,1)S(1)}, bf16[2,256,768]{2,1,0:T(8,128)(2,1)S(1)}, u32[]{:S(2)}, u32[]{:S(2)}) %collective-permute-start) | collective-permute-done | bytes 786464 | tf_op jit(solution)/shard_map/ppermute | solution.py:18
  31.9 6.9 %slice.43 = bf16[2,256,768]{2,1,0:T(8,128)(2,1)S(1)} slice(bf16[2,512,768]{2,1,0:T(8,128)(2,1)} %pad_maximum_fusion), slice={[0:2:1], [0:512:2], [0:768:1]} | slice | bytes 1572864 | tf_op jit(solution)/shard_map/slice | solution.py:52
  38.9 1.8 collective-permute-start.1
  40.7 17.0 %collective-permute-done.1 = bf16[2,256,768]{2,1,0:T(8,128)(2,1)S(1)} collective-permute-done((bf16[2,256,768]{2,1,0:T(8,128)(2,1)S(1)}, bf16[2,256,768]{2,1,0:T(8,128)(2,1)S(1)}, u32[]{:S(2)}, u32[]{:S(2)}) %collective-permute-start.1) | collective-permute-done | bytes 786464 | tf_op jit(solution)/shard_map/ppermute | solution.py:18
  58.9 6.9 %slice.44 = bf16[2,256,768]{2,1,0:T(8,128)(2,1)S(1)} slice(bf16[2,512,768]{2,1,0:T(8,128)(2,1)} %pad_maximum_fusion.1), slice={[0:2:1], [0:512:2], [0:768:1]} | slice | bytes 1572864 | tf_op jit(solution)/shard_map/slice | solution.py:56
  67.4 8.4 %all_gather.6 = bf16[2,32,768]{2,1,0:T(8,128)(2,1)S(1)} all-gather(bf16[2,8,768]{2,1,0:T(8,128)(2,1)S(1)} %slice.45), channel_id=1, replica_groups=mesh['inner'=4,'outer'=8] {'inner'}, dimensions={1}, use_global_device_ids=true | all-gather | bytes 122880 | tf_op jit(solution)/shard_map/all_gather | solution.py:60
  75.8 17.1 %all_gather.7 = bf16[2,256,768]{2,1,0:T(8,128)(2,1)} all-gather(bf16[2,32,768]{2,1,0:T(8,128)(2,1)S(1)} %all_gather.6), channel_id=1, replica_groups=mesh['inner'=4,'outer'=8] {'outer'}, dimensions={1}, use_global_device_ids=true | all-gather | bytes 884736 | tf_op jit(solution)/shard_map/all_gather | solution.py:61
  94.2 208.6 %while.10 = (s32[]{:T(128)}, bf16[12,512,64]{1,2,0:T(8,128)(2,1)}, s32[12]{0:T(128)S(1)}, bf16[512,768]{1,0:T(8,128)(2,1)}, bf16[2,512,768]{2,1,0:T(8,128)(2,1)}...) while((s32[]{:T(128)}, bf16[12,512,64]{1,2,0:T(8,128)(2,1)}, ...), condition=%wide.region_11.0_spmd, body=%wide.region_0.11_spmd.sunk | while | flops 309399552 | bytes 34039680 | solution.py:78
  109.7 1.9 fusion.81
  127.1 1.9 fusion.81
  144.5 1.9 fusion.81
  161.8 1.9 fusion.81
  179.2 1.9 fusion.81
  196.6 1.9 fusion.81
  214.0 1.8 fusion.81
  231.4 1.9 fusion.81
  248.7 1.9 fusion.81
  266.1 1.8 fusion.81
  283.5 1.9 fusion.81
  300.9 1.9 fusion.81
  302.7 2.8 fusion.42
  (301 shorter events, 183.3 us)
Async XLA Ops:
  0.0 302.7 %copy-start = (bf16[768,768]{1,0:T(8,128)(2,1)S(1)}, bf16[768,768]{1,0:T(8,128)(2,1)}, u32[]{:S(2)}) copy-start(bf16[768,768]{1,0:T(8,128)(2,1)} %param.9) | copy-start | bytes 3538948
  10.1 20.5 %collective-permute-start = (bf16[2,256,768]{2,1,0:T(8,128)(2,1)S(1)}, bf16[2,256,768]{2,1,0:T(8,128)(2,1)S(1)}, u32[]{:S(2)}, u32[]{:S(2)}) collective-permute-start(bf16[2,256,768]{2,1,0:T(8,128)(2,1)S(1)} %slice.42), channel_id=1, source_target_pairs={{0,8},{8,0},{16,24},{24,16},{1,9},{9,1},{17,25},{25,17},{2,10},{10... | collective-permute-start | bytes 2359304 | tf_op jit(solution)/shard_map/ppermute | solution.py:18
  38.9 18.8 %collective-permute-start.1 = (bf16[2,256,768]{2,1,0:T(8,128)(2,1)S(1)}, bf16[2,256,768]{2,1,0:T(8,128)(2,1)S(1)}, u32[]{:S(2)}, u32[]{:S(2)}) collective-permute-start(bf16[2,256,768]{2,1,0:T(8,128)(2,1)S(1)} %slice.43), channel_id=1, source_target_pairs={{0,16},{16,0},{8,24},{24,8},{1,17},{17,1},{9,25},{25,9},{2,18},{18... | collective-permute-start | bytes 2359304 | tf_op jit(solution)/shard_map/ppermute | solution.py:18
  65.9 27.1 %collective-permute-start.2 = (bf16[2,256,768]{2,1,0:T(8,128)(2,1)S(1)}, bf16[2,256,768]{2,1,0:T(8,128)(2,1)S(1)}, u32[]{:S(2)}, u32[]{:S(2)}) collective-permute-start(bf16[2,256,768]{2,1,0:T(8,128)(2,1)S(1)} %slice.44), channel_id=1, source_target_pairs={{0,1},{1,0},{2,3},{3,2},{4,5},{5,4},{6,7},{7,6},{8,9},{9,8},{10,11... | collective-permute-start | bytes 2359304 | tf_op jit(solution)/shard_map/ppermute | solution.py:18
  104.4 3.0 copy-start.3
  106.0 2.6 copy-start.5
  121.7 3.0 copy-start.3
  123.4 2.6 copy-start.5
  139.1 3.0 copy-start.3
  140.8 2.6 copy-start.5
  156.5 3.0 copy-start.3
  158.2 2.6 copy-start.5
  173.9 3.0 copy-start.3
  191.3 3.0 copy-start.3
  192.9 2.6 copy-start.5
  208.6 3.0 copy-start.3
  226.0 3.0 copy-start.3
  227.7 2.6 copy-start.5
  243.4 3.0 copy-start.3
  245.1 2.6 copy-start.5
  260.8 3.0 copy-start.3
  278.2 3.0 copy-start.3
  279.8 2.6 copy-start.5
  295.5 3.0 copy-start.3
  (41 other events, 70.3 us)
where the time goes:
time: 309 us; the launch traced here: 306 us
  matrix products  177 us (57%)
  local copies, waits for them, and re-layouts  42.1 us (14%)
  waiting for transfers between devices  34.5 us (11%)
  blocking collectives  25.5 us (8%)
  other arithmetic  12.5 us (4%)
  loops' own time  9.35 us (3%)
  starting transfers between devices  4.91 us (2%)
    dot_general x60, matrix products, head_terms(): jnp.einsum('td,nd->tn', query_part, level_set[0], preferred_element_type=...  88.2 us
    dot_general x60, matrix products, head_terms(): jnp.dot(weights, level_set[1], preferred_element_type=jnp.float32)  85.6 us
    ppermute x3, waiting for transfers between devices, partner_2(): return lax.ppermute(block, axis, route)  34.5 us
    all_gather x1, blocking collectives, local(): global_set = lax.all_gather(inner_set, 'outer', axis=1, tiled=True)  17.1 us
    slice x2, local copies, waits for them, and re-layouts, local(): kv_half = current[:, ::2]  13.8 us
    while x120, local copies, waits for them, and re-layouts  9.68 us
    another operation x1, loops' own time, local(): merged = lax.map(per_head, jnp.arange(HEADS, dtype=jnp.int32))  9.35 us
    reduce_sum x36, other arithmetic, head_terms(): row_total = jnp.sum(expo_rows, axis=1, keepdims=True)  8.56 us
  transfers between devices with their start and end apart: 3, of which 2 were waited for; matrix products, arithmetic and copies ran while one was open for 0% of the time, Pallas kernels for 0%

commit v1 on v0

v1 whole, which is shorter than its diff:
```python
import functools
import math

import jax
import jax.numpy as jnp
import numpy as np
from jax import lax
from jax.experimental import pallas as pl
from jax.experimental.pallas import tpu as pltpu
from jax.sharding import PartitionSpec as P

HEAD_DIM = 64
GSTEP = 64
PAIR = 2 * HEAD_DIM
CHUNK = 256
LOG2E = math.log2(math.e)
VMEM_BYTES = 56 * 1024 * 1024


def across(block, axis, bit):
    count = lax.axis_size(axis)
    return lax.ppermute(block, axis, [(i, i ^ (1 << bit)) for i in range(count)])


def nested_order(tokens, strides):
    rows = np.arange(tokens)
    rank = sum((rows % s == 0).astype(np.int64) for s in strides)
    return np.lexsort((rows, -rank)), rank


def runs(counts):
    found = []
    for at, value in enumerate(counts):
        if found and found[-1][2] == value:
            found[-1][1] = at + 1
        else:
            found.append([at, at + 1, int(value)])
    return [tuple(entry) for entry in found]


def order_rows(select, key_rows, values, prefixes):
    tokens, width = key_rows.shape

    def kernel(select_ref, key_ref, value_ref, all_ref, *prefix_refs):
        for half, ref in enumerate((key_ref, value_ref)):
            moved = jnp.dot(
                select_ref[...], ref[...], preferred_element_type=jnp.float32
            ).astype(jnp.bfloat16)
            cols = slice(half * width, (half + 1) * width)
            all_ref[:, cols] = moved
            for (low, high), prefix_ref in zip(prefixes, prefix_refs):
                prefix_ref[:, cols] = moved[low:high]

    shapes = [(tokens, 2 * width)] + [(high - low, 2 * width) for low, high in prefixes]
    return pl.pallas_call(
        kernel,
        out_shape=[jax.ShapeDtypeStruct(shape, jnp.bfloat16) for shape in shapes],
        compiler_params=pltpu.CompilerParams(vmem_limit_bytes=VMEM_BYTES),
        cost_estimate=pl.CostEstimate(
            flops=4 * tokens * tokens * width, bytes_accessed=10 * tokens * width, transcendentals=0
        ),
    )(select, key_rows, values)


def attend(queries, sets, counts, state=None, out_weight=None):
    tokens, width = queries.shape
    heads, pairs = width // HEAD_DIM, width // PAIR
    sizes = [block.shape[0] for block in sets]
    keys = sum(sizes)
    padded = -(-keys // CHUNK) * CHUNK
    row_runs = runs(counts)
    scale = HEAD_DIM**-0.5 * LOG2E
    final = out_weight is not None
    n_state = 0 if state is None else 3

    def kernel(*refs):
        query_ref, refs = refs[0], refs[1:]
        set_refs, refs = refs[: len(sets)], refs[len(sets) :]
        state_refs, refs = refs[:n_state], refs[n_state:]
        if final:
            weight_ref, out_ref, score_ref, value_ref, attended_ref = refs
        else:
            numer_out, peak_out, total_out, score_ref, value_ref = refs

        ones = jnp.ones((16, padded), jnp.bfloat16)

        def pair_step(pair, carry):
            base = pl.multiple_of(pair * PAIR, PAIR)
            query_pair = query_ref[:, pl.ds(base, PAIR)]
            lane = lax.broadcasted_iota(jnp.int32, query_pair.shape, 1)
            at = 0
            for ref, size in zip(set_refs, sizes):
                value_ref[at : at + size, :] = ref[:, pl.ds(base + width, PAIR)]
                at += size
            if padded > keys:
                value_ref[keys:, :] = jnp.zeros((padded - keys, PAIR), jnp.bfloat16)
            values_t = value_ref[...].T
            for half in range(2):
                head = 2 * pair + half
                own = (lane < HEAD_DIM) if half == 0 else (lane >= HEAD_DIM)
                query_head = jnp.where(own, query_pair, jnp.zeros_like(query_pair))
                running = None
                at = 0
                for ref, size in zip(set_refs, sizes):
                    for low in range(0, size, CHUNK):
                        count = min(CHUNK, size - low)
                        scores = lax.dot_general(
                            ref[low : low + count, pl.ds(base, PAIR)],
                            query_head,
                            (((1,), (1,)), ((), ())),
                            preferred_element_type=jnp.float32,
                        )
                        score_ref[half, at : at + count, :] = scores
                        tallest = jnp.max(scores.reshape(count // 8, 8, tokens), axis=0)
                        running = tallest if running is None else jnp.maximum(running, tallest)
                        at += count
                peak = jnp.max(running, axis=0, keepdims=True) * scale
                if state is not None:
                    before = state_refs[1][pl.ds(head, 1), :]
                    peak = jnp.maximum(peak, before)
                weighted = jnp.concatenate(
                    [values_t[half * HEAD_DIM : (half + 1) * HEAD_DIM], ones], axis=0
                )
                gathered = None
                for low in range(0, padded, CHUNK):
                    high = min(low + CHUNK, keys)
                    pieces = []
                    for first, last, times in row_runs:
                        first, last = max(first, low), min(last, high)
                        if first < last:
                            offset = peak - math.log2(times)
                            pieces.append(
                                jnp.exp2(score_ref[half, first:last, :] * scale - offset)
                            )
                    if low + CHUNK > keys:
                        pieces.append(jnp.zeros((low + CHUNK - keys, tokens), jnp.float32))
                    probs = (
                        pieces[0] if len(pieces) == 1 else jnp.concatenate(pieces, axis=0)
                    ).astype(jnp.bfloat16)
                    product = jnp.dot(
                        weighted[:, low : low + CHUNK], probs, preferred_element_type=jnp.float32
                    )
                    gathered = product if gathered is None else gathered + product
                numer, total = gathered[:HEAD_DIM], gathered[HEAD_DIM : HEAD_DIM + 1]
                rows = pl.ds(pl.multiple_of(base + half * HEAD_DIM, HEAD_DIM), HEAD_DIM)
                if state is not None:
                    factor = jnp.exp2(before - peak)
                    numer = numer + factor * state_refs[0][rows, :]
                    total = total + factor * state_refs[2][pl.ds(head, 1), :]
                if final:
                    attended_ref[rows, :] = (numer / total).astype(jnp.bfloat16)
                else:
                    numer_out[rows, :] = numer
                    peak_out[pl.ds(head, 1), :] = peak
                    total_out[pl.ds(head, 1), :] = total
            return carry

        lax.fori_loop(0, pairs, pair_step, 0)
        if final:
            out_ref[...] = lax.dot_general(
                attended_ref[...],
                weight_ref[...],
                (((0,), (0,)), ((), ())),
                preferred_element_type=jnp.float32,
            ).astype(jnp.bfloat16)

    if final:
        out_shape = jax.ShapeDtypeStruct((tokens, width), jnp.bfloat16)
    else:
        out_shape = [
            jax.ShapeDtypeStruct((width, tokens), jnp.float32),
            jax.ShapeDtypeStruct((heads, tokens), jnp.float32),
            jax.ShapeDtypeStruct((heads, tokens), jnp.float32),
        ]
    scratch = [
        pltpu.VMEM((2, padded, tokens), jnp.float32),
        pltpu.VMEM((padded, PAIR), jnp.bfloat16),
    ]
    if final:
        scratch.append(pltpu.VMEM((width, tokens), jnp.bfloat16))
    operands = [queries, *sets, *(state or []), *([out_weight] if final else [])]
    return pl.pallas_call(
        kernel,
        out_shape=out_shape,
        scratch_shapes=scratch,
        compiler_params=pltpu.CompilerParams(vmem_limit_bytes=VMEM_BYTES),
        cost_estimate=pl.CostEstimate(
            flops=16 * tokens * keys * width,
            bytes_accessed=4 * keys * width + 4 * tokens * width,
            transcendentals=tokens * keys * heads,
        ),
    )(*operands)


def local(queries, key_rows, values, out_weight):
    query_rows = queries[0]
    tokens = query_rows.shape[0]
    inner_bits = lax.axis_size("inner").bit_length() - 1
    outer_bits = lax.axis_size("outer").bit_length() - 1
    strides = [1 << (bit + 1) for bit in range(inner_bits + 1)] + [GSTEP]
    order, rank = nested_order(tokens, strides)
    select = np.zeros((tokens, tokens), np.float32)
    select[np.arange(tokens), order] = 1.0

    def prefix_counts(level, length):
        used = strides[level:]
        return sum((order[:length] % s == 0).astype(np.int64) for s in used)

    sends = [tokens >> (bit + 1) for bit in range(inner_bits + 1)]
    n_global = tokens // GSTEP
    prefixes = [(0, sends[1]), (sends[1], sends[0])]
    prefixes += [(0, count) for count in sends[1:]] + [(0, n_global)]
    ordered = order_rows(jnp.asarray(select, jnp.bfloat16), key_rows[0], values[0], prefixes)
    own, first_a, first_b = ordered[:3]
    own_sends, own_global = ordered[3:-1], ordered[-1]

    near_a = across(first_a, "inner", 0)
    direct = [across(own_sends[bit - 1], "inner", bit) for bit in range(1, inner_bits)]
    far = own_global
    far_parts = []
    for bit in range(1, outer_bits):
        came = across(far, "outer", bit)
        far = jnp.concatenate([far, came], axis=0)
    far = far[n_global:]
    near_b = across(first_b, "inner", 0)
    far = jnp.concatenate([far, across(far, "inner", 0)], axis=0)

    state = attend(query_rows, [own], 1 + rank[order])

    sets, counts = [near_a, near_b], [prefix_counts(0, sends[0])]
    held = [near_a]
    for bit in range(1, inner_bits):
        count = sends[bit]
        moved = jnp.concatenate([block[:count] for block in held] + [far], axis=0)
        came = across(moved, "inner", bit)
        sets += [direct[bit - 1], came]
        n_held = len(held) * count
        counts += [prefix_counts(bit, count)] * (1 + len(held))
        counts.append(np.ones(far.shape[0], np.int64))
        held = held + [direct[bit - 1]] + [
            came[at : at + count] for at in range(0, n_held, count)
        ]
        far = jnp.concatenate([far, came[n_held:]], axis=0)
    count = sends[inner_bits]
    moved = jnp.concatenate(
        [own_sends[inner_bits - 1]] + [block[:count] for block in held] + [far], axis=0
    )
    came = across(moved, "outer", 0)
    sets.append(came)
    counts += [prefix_counts(inner_bits, count)] * (1 + len(held))
    counts.append(np.ones(far.shape[0], np.int64))
    n_near = far.shape[0] >> (inner_bits - 1) if inner_bits > 1 else far.shape[0]
    sets.append(far[:n_near])
    counts.append(np.ones(n_near, np.int64))

    result = attend(query_rows, sets, np.concatenate(counts), state, out_weight)
    return result[None]


def solution(mesh):
    placed = (P("outer", "inner", None), P("outer", "inner", None), P("outer", "inner", None), P())
    return jax.shard_map(
        local, mesh=mesh, in_specs=placed, out_specs=P("outer", "inner", None), check_vma=False
    )
```

time: 309 us -> 66.5 us (0.22); the launches traced: 306 us -> 66.3 us
  matrix products: 177 us -> 0 us
  local copies, waits for them, and re-layouts: 42.1 us -> 2.13 us
  Pallas kernels: 0 us -> 30.9 us
  blocking collectives: 25.5 us -> 0 us
  waiting for transfers between devices: 34.5 us -> 18.5 us
  other arithmetic: 12.5 us -> 1.47 us
  loops' own time: 9.35 us -> 0 us
  starting transfers between devices: 4.91 us -> 13.2 us
    dot_general x121 -> x0, matrix products: 177 us -> none  [the longest x60 88.2 us: head_terms(): jnp.einsum('td,nd->tn', query_part, level_set[0], preferred_element_type=...]
    pallas_call x0 -> x3, Pallas kernels: none -> 30.9 us  [the longest x2 26.9 us: attend(): pl.pallas_call(kernel, out_shape=out_shape, scratch_shapes=scratch, compi...]
    all_gather x2 -> x0, blocking collectives: 25.5 us -> none  [the longest x1 17.1 us: local(): global_set = lax.all_gather(inner_set, 'outer', axis=1, tiled=True)]
    slice x4 -> x0, local copies, waits for them, and re-layouts: 22.2 us -> none  [the longest x2 13.8 us: local(): kv_half = current[:, ::2]]
    ppermute x3 -> x8, waiting for transfers between devices: 34.5 us -> 18.5 us  [across(): return lax.ppermute(block, axis, [(i, i ^ 1 << bit) for i in range(count)])]
    while x120 -> x0, local copies, waits for them, and re-layouts: 9.68 us -> none
    another operation x1 -> x0, loops' own time: 9.35 us -> none  [local(): merged = lax.map(per_head, jnp.arange(HEADS, dtype=jnp.int32))]
    reduce_sum x36 -> x0, other arithmetic: 8.56 us -> none  [head_terms(): row_total = jnp.sum(expo_rows, axis=1, keepdims=True)]
  transfers between devices with their start and end apart: 3 -> 8, of which waited for: 2 -> 3; matrix products, arithmetic and copies ran while one was open for 0% -> 3% of each run, Pallas kernels for 0% -> 15%
where the time goes in v1:
time: 66.5 us; the launch traced here: 66.3 us
  Pallas kernels  30.9 us (46%)
  waiting for transfers between devices  18.5 us (28%)
  starting transfers between devices  13.2 us (20%)
  local copies, waits for them, and re-layouts  2.13 us (3%)
  other arithmetic  1.47 us (2%)
    pallas_call x2, Pallas kernels, attend(): pl.pallas_call(kernel, out_shape=out_shape, scratch_shapes=scratch, compi...  26.9 us
    ppermute x8, waiting for transfers between devices, across(): return lax.ppermute(block, axis, [(i, i ^ 1 << bit) for i in range(count)])  18.5 us
    ppermute x8, starting transfers between devices, across(): return lax.ppermute(block, axis, [(i, i ^ 1 << bit) for i in range(count)])  13.2 us
    pallas_call x1, Pallas kernels, order_rows(): pl.pallas_call(kernel, out_shape=[jax.ShapeDtypeStruct(shape, jnp.bfloat1...  4.03 us
    unnamed x19, local copies, waits for them, and re-layouts  2.12 us
  transfers between devices with their start and end apart: 8, of which 3 were waited for; matrix products, arithmetic and copies ran while one was open for 3% of the time, Pallas kernels for 15%

profile of v1, /device:TPU:0, one launch (start us, length us, event | category | flops | bytes accessed | tf_op | source)
XLA Modules:
  0.0 66.3 jit_solution(6818484470101148449)
XLA Ops:
  0.0 4.0 %shard_map.55 = (bf16[512,1536]{1,0:T(8,128)(2,1)}, bf16[128,1536]{1,0:T(8,128)(2,1)}, bf16[128,1536]{1,0:T(8,128)(2,1)}, bf16[128,1536]{1,0:T(8,128)(2,1)}, bf1...) custom-call(bf16[512,512]{1,0:T(8,128)(2,1)} %constant.2.clone.select_ref, bf16[512,768]{1,0:T(8,128)(2,1)} %bitcast.4, ...), custom_call_target="tpu_custom_call" | custom-call | flops 805306368 | bytes 3932160 | tf_op jit(solution)/shard_map/pallas_call | solution.py:55
  4.0 3.0 %collective-permute-start.3 = (bf16[8,1536]{1,0:T(8,128)(2,1)}, bf16[8,1536]{1,0:T(8,128)(2,1)S(1)}, u32[]{:S(2)}, u32[]{:S(2)}) collective-permute-start(bf16[8,1536]{1,0:T(8,128)(2,1)} %get-tuple-element.17), channel_id=1, source_target_pairs={{0,2},{1,3},{2,0},{3,1},{4,6},{5,7},{6,4},{7,5},{8,10},{9,11},{10,... | collective-permute-start | bytes 73736 | tf_op jit(solution)/shard_map/ppermute | solution.py:22
  7.1 2.0 %collective-permute-done.3 = bf16[8,1536]{1,0:T(8,128)(2,1)S(1)} collective-permute-done((bf16[8,1536]{1,0:T(8,128)(2,1)}, bf16[8,1536]{1,0:T(8,128)(2,1)S(1)}, u32[]{:S(2)}, u32[]{:S(2)}) %collective-permute-start.3) | collective-permute-done | bytes 24608 | tf_op jit(solution)/shard_map/ppermute | solution.py:22
  9.1 0.7 %pad_maximum_fusion.3 = bf16[16,1536]{1,0:T(8,128)(2,1)S(1)} fusion(bf16[8,1536]{1,0:T(8,128)(2,1)S(1)} %collective-permute-done.3, bf16[8,1536]{1,0:T(8,128)(2,1)} %get-tuple-element.17), kind=kLoop, calls=%fused_computation.7 | loop fusion | flops 98304 | bytes 98304 | tf_op jit(solution)/shard_map/concatenate | solution.py:223
  9.8 3.0 %collective-permute-start.4 = (bf16[16,1536]{1,0:T(8,128)(2,1)S(1)}, bf16[16,1536]{1,0:T(8,128)(2,1)S(1)}, u32[]{:S(2)}, u32[]{:S(2)}) collective-permute-start(bf16[16,1536]{1,0:T(8,128)(2,1)S(1)} %pad_maximum_fusion.3), channel_id=1, source_target_pairs={{0,4},{1,5},{2,6},{3,7},{4,0},{5,1},{6,2},{7,3},{8,12},{9,13},{10,... | collective-permute-start | bytes 147464 | tf_op jit(solution)/shard_map/ppermute | solution.py:22
  12.9 1.5 %collective-permute-start = (bf16[128,1536]{1,0:T(8,128)(2,1)}, bf16[128,1536]{1,0:T(8,128)(2,1)S(1)}, u32[]{:S(2)}, u32[]{:S(2)}) collective-permute-start(bf16[128,1536]{1,0:T(8,128)(2,1)} %get-tuple-element.14), channel_id=1, source_target_pairs={{0,8},{8,0},{16,24},{24,16},{1,9},{9,1},{17,25},{25,17},{2,10},{10... | collective-permute-start | bytes 1179656 | tf_op jit(solution)/shard_map/ppermute | solution.py:22
  14.3 1.5 %collective-permute-start.2 = (bf16[128,1536]{1,0:T(8,128)(2,1)}, bf16[128,1536]{1,0:T(8,128)(2,1)S(1)}, u32[]{:S(2)}, u32[]{:S(2)}) collective-permute-start(bf16[128,1536]{1,0:T(8,128)(2,1)} %get-tuple-element.16), channel_id=1, source_target_pairs={{0,16},{8,24},{16,0},{24,8},{1,17},{9,25},{17,1},{25,9},{2,18},{10... | collective-permute-start | bytes 1179656 | tf_op jit(solution)/shard_map/ppermute | solution.py:22
  15.9 0.0 collective-permute-done.4
  15.9 0.9 %collective-permute-start.5 = (bf16[24,1536]{1,0:T(8,128)(2,1)S(1)}, bf16[24,1536]{1,0:T(8,128)(2,1)S(1)}, u32[]{:S(2)}, u32[]{:S(2)}) collective-permute-start(bf16[24,1536]{1,0:T(8,128)(2,1)S(1)} %pad_maximum_fusion.2), channel_id=1, source_target_pairs={{0,8},{8,0},{16,24},{24,16},{1,9},{9,1},{17,25},{25,17},{2,10},{10... | collective-permute-start | bytes 221192 | tf_op jit(solution)/shard_map/ppermute | solution.py:22
  16.7 0.9 %constant_dynamic-update-slice_fusion.3 = bf16[352,1536]{1,0:T(8,128)(2,1)S(1)} fusion(bf16[64,1536]{1,0:T(8,128)(2,1)} %get-tuple-element.18), kind=kLoop, calls=%fused_computation.11 | loop fusion | bytes 393216
  17.7 6.4 %collective-permute-done.5 = bf16[24,1536]{1,0:T(8,128)(2,1)S(1)} collective-permute-done((bf16[24,1536]{1,0:T(8,128)(2,1)S(1)}, bf16[24,1536]{1,0:T(8,128)(2,1)S(1)}, u32[]{:S(2)}, u32[]{:S(2)}) %collective-permute-start.5) | collective-permute-done | bytes 73760 | tf_op jit(solution)/shard_map/ppermute | solution.py:22
  24.1 0.0 collective-permute-done.refs_1_
  24.1 1.6 %collective-permute-start.6 = (bf16[176,1536]{1,0:T(8,128)(2,1)S(1)}, bf16[176,1536]{1,0:T(8,128)(2,1)S(1)}, u32[]{:S(2)}, u32[]{:S(2)}) collective-permute-start(bf16[176,1536]{1,0:T(8,128)(2,1)S(1)} %pad_maximum_fusion), channel_id=1, source_target_pairs={{0,16},{8,24},{16,0},{24,8},{1,17},{9,25},{17,1},{25,9},{2,18},{10... | collective-permute-start | bytes 1622024 | tf_op jit(solution)/shard_map/ppermute | solution.py:22
  25.7 0.0 collective-permute-done.2.refs_3_
  25.8 10.1 %collective-permute-done.6.refs_4_ = bf16[176,1536]{1,0:T(8,128)(2,1)S(1)} collective-permute-done((bf16[176,1536]{1,0:T(8,128)(2,1)S(1)}, bf16[176,1536]{1,0:T(8,128)(2,1)S(1)}, u32[]{:S(2)}, u32[]{:S(2)}) %collective-permute-start.6) | collective-permute-done | bytes 540704 | tf_op jit(solution)/shard_map/ppermute | solution.py:22
  35.9 0.1 collective-permute-start.7
  36.0 1.6 %collective-permute-start.1 = (bf16[128,1536]{1,0:T(8,128)(2,1)S(1)}, bf16[128,1536]{1,0:T(8,128)(2,1)S(1)}, u32[]{:S(2)}, u32[]{:S(2)}) collective-permute-start(bf16[128,1536]{1,0:T(8,128)(2,1)S(1)} %copy-done.4), channel_id=1, source_target_pairs={{0,8},{8,0},{16,24},{24,16},{1,9},{9,1},{17,25},{25,17},{2,10},{10... | collective-permute-start | bytes 1179656 | tf_op jit(solution)/shard_map/ppermute | solution.py:22
  37.6 10.3 %shard_map.56 = (f32[768,512]{1,0:T(8,128)}, f32[12,512]{1,0:T(8,128)}, f32[12,512]{1,0:T(8,128)}) custom-call(bf16[512,768]{1,0:T(8,128)(2,1)} %bitcast.6, bf16[512,1536]{1,0:T(8,128)(2,1)} %get-tuple-element.19.refs_1_), custom_call_target="tpu_custom_call" | custom-call | flops 3221225472 | bytes 3145728 | tf_op jit(solution)/shard_map/pallas_call | solution.py:182
  47.9 0.7 %pad_maximum_fusion.1.refs_6_ = bf16[48,1536]{1,0:T(8,128)(2,1)} fusion(bf16[24,1536]{1,0:T(8,128)(2,1)S(1)} %collective-permute-done.5, bf16[16,1536]{1,0:T(8,128)(2,1)S(1)} %collective-permute-done.4, bf16[8,1536]{1,0:T(8,128)(2,1)S(1)} %collective-permute-done.3), kind=kLoop, calls=%fused_computation.5 | loop fusion | flops 442368 | bytes 294912 | tf_op jit(solution)/shard_map/concatenate | solution.py:226
  48.6 0.0 collective-permute-done.1.refs_2_
  48.6 0.0 collective-permute-done.7.refs_5_
  48.6 0.7 %copy-done.5 = bf16[128,1536]{1,0:T(8,128)(2,1)} copy-done((bf16[128,1536]{1,0:T(8,128)(2,1)}, bf16[128,1536]{1,0:T(8,128)(2,1)S(1)}, u32[]{:S(2)}) %copy-start.5) | copy-done | bytes 393240
  49.3 0.4 copy-done.3
  49.7 16.6 %shard_map.57 = bf16[512,768]{1,0:T(8,128)(2,1)} custom-call(bf16[512,768]{1,0:T(8,128)(2,1)} %bitcast.7, bf16[128,1536]{1,0:T(8,128)(2,1)} %copy-done, bf16[128,1536]{1,0:T(8,128)(2,1)} %copy-done.5, bf16[128,1536]{1,0:T(8,128)(2,1)} %copy-done.2, bf16[176,1536]{1,0:T(8,128)(2,1)} %copy-done.1, bf16[352,1536]{1,0:T(8,128)(2,1)} %copy-done.3, ...), custom_call_target="tpu_custom_call" | custom-call | flops 6039797760 | bytes 4521984 | tf_op jit(solution)/shard_map/pallas_call | solution.py:182
  (19 shorter events, 0.1 us)
Async XLA Ops:
  4.0 5.0 %collective-permute-start.3 = (bf16[8,1536]{1,0:T(8,128)(2,1)}, bf16[8,1536]{1,0:T(8,128)(2,1)S(1)}, u32[]{:S(2)}, u32[]{:S(2)}) collective-permute-start(bf16[8,1536]{1,0:T(8,128)(2,1)} %get-tuple-element.17), channel_id=1, source_target_pairs={{0,2},{1,3},{2,0},{3,1},{4,6},{5,7},{6,4},{7,5},{8,10},{9,11},{10,... | collective-permute-start | bytes 73736 | tf_op jit(solution)/shard_map/ppermute | solution.py:22
  9.8 6.0 %collective-permute-start.4 = (bf16[16,1536]{1,0:T(8,128)(2,1)S(1)}, bf16[16,1536]{1,0:T(8,128)(2,1)S(1)}, u32[]{:S(2)}, u32[]{:S(2)}) collective-permute-start(bf16[16,1536]{1,0:T(8,128)(2,1)S(1)} %pad_maximum_fusion.3), channel_id=1, source_target_pairs={{0,4},{1,5},{2,6},{3,7},{4,0},{5,1},{6,2},{7,3},{8,12},{9,13},{10,... | collective-permute-start | bytes 147464 | tf_op jit(solution)/shard_map/ppermute | solution.py:22
  12.9 11.2 %collective-permute-start = (bf16[128,1536]{1,0:T(8,128)(2,1)}, bf16[128,1536]{1,0:T(8,128)(2,1)S(1)}, u32[]{:S(2)}, u32[]{:S(2)}) collective-permute-start(bf16[128,1536]{1,0:T(8,128)(2,1)} %get-tuple-element.14), channel_id=1, source_target_pairs={{0,8},{8,0},{16,24},{24,16},{1,9},{9,1},{17,25},{25,17},{2,10},{10... | collective-permute-start | bytes 1179656 | tf_op jit(solution)/shard_map/ppermute | solution.py:22
  14.3 11.4 %collective-permute-start.2 = (bf16[128,1536]{1,0:T(8,128)(2,1)}, bf16[128,1536]{1,0:T(8,128)(2,1)S(1)}, u32[]{:S(2)}, u32[]{:S(2)}) collective-permute-start(bf16[128,1536]{1,0:T(8,128)(2,1)} %get-tuple-element.16), channel_id=1, source_target_pairs={{0,16},{8,24},{16,0},{24,8},{1,17},{9,25},{17,1},{25,9},{2,18},{10... | collective-permute-start | bytes 1179656 | tf_op jit(solution)/shard_map/ppermute | solution.py:22
  15.9 8.2 %collective-permute-start.5 = (bf16[24,1536]{1,0:T(8,128)(2,1)S(1)}, bf16[24,1536]{1,0:T(8,128)(2,1)S(1)}, u32[]{:S(2)}, u32[]{:S(2)}) collective-permute-start(bf16[24,1536]{1,0:T(8,128)(2,1)S(1)} %pad_maximum_fusion.2), channel_id=1, source_target_pairs={{0,8},{8,0},{16,24},{24,16},{1,9},{9,1},{17,25},{25,17},{2,10},{10... | collective-permute-start | bytes 221192 | tf_op jit(solution)/shard_map/ppermute | solution.py:22
  24.1 11.8 %copy-start = (bf16[128,1536]{1,0:T(8,128)(2,1)}, bf16[128,1536]{1,0:T(8,128)(2,1)S(1)}, u32[]{:S(2)}) copy-start(bf16[128,1536]{1,0:T(8,128)(2,1)S(1)} %collective-permute-done.refs_1_) | copy-start | bytes 1179652
  24.1 11.9 %copy-start.4 = (bf16[128,1536]{1,0:T(8,128)(2,1)S(1)}, bf16[128,1536]{1,0:T(8,128)(2,1)}, u32[]{:S(2)}) copy-start(bf16[128,1536]{1,0:T(8,128)(2,1)} %get-tuple-element.15) | copy-start | bytes 1179652
  24.1 11.7 %collective-permute-start.6 = (bf16[176,1536]{1,0:T(8,128)(2,1)S(1)}, bf16[176,1536]{1,0:T(8,128)(2,1)S(1)}, u32[]{:S(2)}, u32[]{:S(2)}) collective-permute-start(bf16[176,1536]{1,0:T(8,128)(2,1)S(1)} %pad_maximum_fusion), channel_id=1, source_target_pairs={{0,16},{8,24},{16,0},{24,8},{1,17},{9,25},{17,1},{25,9},{2,18},{10... | collective-permute-start | bytes 1622024 | tf_op jit(solution)/shard_map/ppermute | solution.py:22
  25.7 22.1 %copy-start.2 = (bf16[128,1536]{1,0:T(8,128)(2,1)}, bf16[128,1536]{1,0:T(8,128)(2,1)S(1)}, u32[]{:S(2)}) copy-start(bf16[128,1536]{1,0:T(8,128)(2,1)S(1)} %collective-permute-done.2.refs_3_) | copy-start | bytes 1179652
  35.9 12.0 %copy-start.1 = (bf16[176,1536]{1,0:T(8,128)(2,1)}, bf16[176,1536]{1,0:T(8,128)(2,1)S(1)}, u32[]{:S(2)}) copy-start(bf16[176,1536]{1,0:T(8,128)(2,1)S(1)} %collective-permute-done.6.refs_4_) | copy-start | bytes 1622020
  35.9 12.6 %collective-permute-start.7 = (bf16[352,1536]{1,0:T(8,128)(2,1)S(1)}, bf16[352,1536]{1,0:T(8,128)(2,1)S(1)}, u32[]{:S(2)}, u32[]{:S(2)}) collective-permute-start(bf16[352,1536]{1,0:T(8,128)(2,1)S(1)} %slice_dynamic-update-slice_fusion.3), channel_id=1, source_target_pairs={{0,1},{1,0},{2,3},{3,2},{4,5},{5,4},{6,7},{7,6},{8,9},{9,8},{10,11... | collective-permute-start | bytes 3244040 | tf_op jit(solution)/shard_map/ppermute | solution.py:22
  36.0 12.5 %collective-permute-start.1 = (bf16[128,1536]{1,0:T(8,128)(2,1)S(1)}, bf16[128,1536]{1,0:T(8,128)(2,1)S(1)}, u32[]{:S(2)}, u32[]{:S(2)}) collective-permute-start(bf16[128,1536]{1,0:T(8,128)(2,1)S(1)} %copy-done.4), channel_id=1, source_target_pairs={{0,8},{8,0},{16,24},{24,16},{1,9},{9,1},{17,25},{25,17},{2,10},{10... | collective-permute-start | bytes 1179656 | tf_op jit(solution)/shard_map/ppermute | solution.py:22
  48.6 0.8 %copy-start.5 = (bf16[128,1536]{1,0:T(8,128)(2,1)}, bf16[128,1536]{1,0:T(8,128)(2,1)S(1)}, u32[]{:S(2)}) copy-start(bf16[128,1536]{1,0:T(8,128)(2,1)S(1)} %collective-permute-done.1.refs_2_) | copy-start | bytes 1179652
  48.6 1.1 %copy-start.3 = (bf16[352,1536]{1,0:T(8,128)(2,1)}, bf16[352,1536]{1,0:T(8,128)(2,1)S(1)}, u32[]{:S(2)}) copy-start(bf16[352,1536]{1,0:T(8,128)(2,1)S(1)} %collective-permute-done.7.refs_5_) | copy-start | bytes 3244036

commit v2 on v1

--- a/solution.py
+++ b/solution.py
@@ -83,79 +83,106 @@
             numer_out, peak_out, total_out, score_ref, value_ref = refs
 
         ones = jnp.ones((16, padded), jnp.bfloat16)
-
-        def pair_step(pair, carry):
-            base = pl.multiple_of(pair * PAIR, PAIR)
-            query_pair = query_ref[:, pl.ds(base, PAIR)]
-            lane = lax.broadcasted_iota(jnp.int32, query_pair.shape, 1)
+        key_chunks = []
+        at = 0
+        for ref, size in zip(set_refs, sizes):
+            for low in range(0, size, CHUNK):
+                count = min(CHUNK, size - low)
+                key_chunks.append((ref, low, count, at))
+                at += count
+        value_chunks = list(range(0, padded, CHUNK))
+
+        def column(pair):
+            return pl.multiple_of(pair * PAIR, PAIR)
+
+        def head_queries(pair, half):
+            turned = query_ref[:, pl.ds(column(pair), PAIR)].T
+            row = lax.broadcasted_iota(jnp.int32, turned.shape, 0)
+            own = (row < HEAD_DIM) if half == 0 else (row >= HEAD_DIM)
+            return jnp.where(own, turned, jnp.zeros_like(turned))
+
+        def score(pair, half, query_head, chunk, running):
+            ref, low, count, at = chunk
+            scores = jnp.dot(
+                ref[low : low + count, pl.ds(column(pair), PAIR)],
+                query_head,
+                preferred_element_type=jnp.float32,
+            )
+            score_ref[half, at : at + count, :] = scores
+            tallest = jnp.max(scores.reshape(count // 8, 8, tokens), axis=0)
+            return tallest if running is None else jnp.maximum(running, tallest)
+
+        def weigh(half, peak, weighted, low, gathered):
+            high = min(low + CHUNK, keys)
+            pieces = []
+            for first, last, times in row_runs:
+                first, last = max(first, low), min(last, high)
+                if first < last:
+                    offset = peak - math.log2(times)
+                    pieces.append(jnp.exp2(score_ref[half, first:last, :] * scale - offset))
+            if low + CHUNK > keys:
+                pieces.append(jnp.zeros((low + CHUNK - keys, tokens), jnp.float32))
+            probs = (pieces[0] if len(pieces) == 1 else jnp.concatenate(pieces, axis=0)).astype(
+                jnp.bfloat16
+            )
+            product = jnp.dot(
+                weighted[:, low : low + CHUNK], probs, preferred_element_type=jnp.float32
+            )
+            return product if gathered is None else gathered + product
+
+        def finish(pair, half, gathered, peak, before):
+            head = 2 * pair + half
+            numer, total = gathered[:HEAD_DIM], gathered[HEAD_DIM : HEAD_DIM + 1]
+            rows = pl.ds(pl.multiple_of(column(pair) + half * HEAD_DIM, HEAD_DIM), HEAD_DIM)
+            if state is not None:
+                factor = jnp.exp2(before - peak)
+                numer = numer + factor * state_refs[0][rows, :]
+                total = total + factor * state_refs[2][pl.ds(head, 1), :]
+            if final:
+                attended_ref[rows, :] = (numer / total).astype(jnp.bfloat16)
+            else:
+                numer_out[rows, :] = numer
+                peak_out[pl.ds(head, 1), :] = peak
+                total_out[pl.ds(head, 1), :] = total
+
+        def overlap(pair, half, running, values_t, next_pair, next_half):
+            peak = jnp.max(running, axis=0, keepdims=True) * scale
+            before = None
+            if state is not None:
+                before = state_refs[1][pl.ds(2 * pair + half, 1), :]
+                peak = jnp.maximum(peak, before)
+            weighted = jnp.concatenate(
+                [values_t[half * HEAD_DIM : (half + 1) * HEAD_DIM], ones], axis=0
+            )
+            query_head = head_queries(next_pair, next_half)
+            next_running, gathered = None, None
+            for step in range(max(len(key_chunks), len(value_chunks))):
+                if step < len(key_chunks):
+                    next_running = score(
+                        next_pair, next_half, query_head, key_chunks[step], next_running
+                    )
+                if step < len(value_chunks):
+                    gathered = weigh(half, peak, weighted, value_chunks[step], gathered)
+            finish(pair, half, gathered, peak, before)
+            return next_running
+
+        def pair_step(pair, running):
             at = 0
             for ref, size in zip(set_refs, sizes):
-                value_ref[at : at + size, :] = ref[:, pl.ds(base + width, PAIR)]
+                value_ref[at : at + size, :] = ref[:, pl.ds(column(pair) + width, PAIR)]
                 at += size
             if padded > keys:
                 value_ref[keys:, :] = jnp.zeros((padded - keys, PAIR), jnp.bfloat16)
             values_t = value_ref[...].T
-            for half in range(2):
-                head = 2 * pair + half
-                own = (lane < HEAD_DIM) if half == 0 else (lane >= HEAD_DIM)
-                query_head = jnp.where(own, query_pair, jnp.zeros_like(query_pair))
-                running = None
-                at = 0
-                for ref, size in zip(set_refs, sizes):
-                    for low in range(0, size, CHUNK):
-                        count = min(CHUNK, size - low)
-                        scores = lax.dot_general(
-                            ref[low : low + count, pl.ds(base, PAIR)],
-                            query_head,
-                            (((1,), (1,)), ((), ())),
-                            preferred_element_type=jnp.float32,
-                        )
-                        score_ref[half, at : at + count, :] = scores
-                        tallest = jnp.max(scores.reshape(count // 8, 8, tokens), axis=0)
-                        running = tallest if running is None else jnp.maximum(running, tallest)
-                        at += count
-                peak = jnp.max(running, axis=0, keepdims=True) * scale
-                if state is not None:
-                    before = state_refs[1][pl.ds(head, 1), :]
-                    peak = jnp.maximum(peak, before)
-                weighted = jnp.concatenate(
-                    [values_t[half * HEAD_DIM : (half + 1) * HEAD_DIM], ones], axis=0
-                )
-                gathered = None
-                for low in range(0, padded, CHUNK):
-                    high = min(low + CHUNK, keys)
-                    pieces = []
-                    for first, last, times in row_runs:
-                        first, last = max(first, low), min(last, high)
-                        if first < last:
-                            offset = peak - math.log2(times)
-                            pieces.append(
-                                jnp.exp2(score_ref[half, first:last, :] * scale - offset)
-                            )
-                    if low + CHUNK > keys:
-                        pieces.append(jnp.zeros((low + CHUNK - keys, tokens), jnp.float32))
-                    probs = (
-                        pieces[0] if len(pieces) == 1 else jnp.concatenate(pieces, axis=0)
-                    ).astype(jnp.bfloat16)
-                    product = jnp.dot(
-                        weighted[:, low : low + CHUNK], probs, preferred_element_type=jnp.float32
-                    )
-                    gathered = product if gathered is None else gathered + product
-                numer, total = gathered[:HEAD_DIM], gathered[HEAD_DIM : HEAD_DIM + 1]
-                rows = pl.ds(pl.multiple_of(base + half * HEAD_DIM, HEAD_DIM), HEAD_DIM)
-                if state is not None:
-                    factor = jnp.exp2(before - peak)
-                    numer = numer + factor * state_refs[0][rows, :]
-                    total = total + factor * state_refs[2][pl.ds(head, 1), :]
-                if final:
-                    attended_ref[rows, :] = (numer / total).astype(jnp.bfloat16)
-                else:
-                    numer_out[rows, :] = numer
-                    peak_out[pl.ds(head, 1), :] = peak
-                    total_out[pl.ds(head, 1), :] = total
-            return carry
-
-        lax.fori_loop(0, pairs, pair_step, 0)
+            running = overlap(pair, 0, running, values_t, pair, 1)
+            later = jnp.minimum(pair + 1, pairs - 1)
+            return overlap(pair, 1, running, values_t, later, 0)
+
+        first_head = head_queries(0, 0)
+        running = None
+        for chunk in key_chunks:
+            running = score(0, 0, first_head, chunk, running)
+        lax.fori_loop(0, pairs, pair_step, running)
         if final:
             out_ref[...] = lax.dot_general(
                 attended_ref[...],

time: 66.5 us -> 61.2 us (0.920)
  Pallas kernels: 30.9 us -> 23.6 us
  waiting for transfers between devices: 18.5 us -> 20.5 us
    pallas_call x2, Pallas kernels: 26.9 us -> 19.5 us  [attend(): pl.pallas_call(kernel, out_shape=out_shape, scratch_shapes=scratch, compi...]
    ppermute x8, waiting for transfers between devices: 18.5 us -> 20.5 us  [across(): return lax.ppermute(block, axis, [(i, i ^ 1 << bit) for i in range(count)])]
  transfers between devices with their start and end apart: 8 -> 8, of which waited for: 3 -> 4; matrix products, arithmetic and copies ran while one was open for 3% -> 3% of each run, Pallas kernels for 15% -> 12%
where the time goes in v2:
time: 61.2 us; the launch traced here: 60.9 us
  Pallas kernels  23.6 us (39%)
  waiting for transfers between devices  20.5 us (33%)
  starting transfers between devices  13.2 us (22%)
  local copies, waits for them, and re-layouts  2.14 us (3%)
  other arithmetic  1.47 us (2%)
    ppermute x8, waiting for transfers between devices, across(): return lax.ppermute(block, axis, [(i, i ^ 1 << bit) for i in range(count)])  20.5 us
    pallas_call x2, Pallas kernels, attend(): pl.pallas_call(kernel, out_shape=out_shape, scratch_shapes=scratch, compi...  19.5 us
    ppermute x8, starting transfers between devices, across(): return lax.ppermute(block, axis, [(i, i ^ 1 << bit) for i in range(count)])  13.2 us
    pallas_call x1, Pallas kernels, order_rows(): pl.pallas_call(kernel, out_shape=[jax.ShapeDtypeStruct(shape, jnp.bfloat1...  4.03 us
    unnamed x19, local copies, waits for them, and re-layouts  2.13 us
  transfers between devices with their start and end apart: 8, of which 4 were waited for; matrix products, arithmetic and copies ran while one was open for 3% of the time, Pallas kernels for 12%

profile of v2, /device:TPU:0, one launch (start us, length us, event | category | flops | bytes accessed | tf_op | source)
XLA Modules:
  0.0 60.9 jit_solution(1182573491842940323)
XLA Ops:
  0.0 4.0 %shard_map.55 = (bf16[512,1536]{1,0:T(8,128)(2,1)}, bf16[128,1536]{1,0:T(8,128)(2,1)}, bf16[128,1536]{1,0:T(8,128)(2,1)}, bf16[128,1536]{1,0:T(8,128)(2,1)}, bf1...) custom-call(bf16[512,512]{1,0:T(8,128)(2,1)} %constant.2.clone.select_ref, bf16[512,768]{1,0:T(8,128)(2,1)} %bitcast.4, ...), custom_call_target="tpu_custom_call" | custom-call | flops 805306368 | bytes 3932160 | tf_op jit(solution)/shard_map/pallas_call | solution.py:55
  4.0 3.0 %collective-permute-start.3 = (bf16[8,1536]{1,0:T(8,128)(2,1)}, bf16[8,1536]{1,0:T(8,128)(2,1)S(1)}, u32[]{:S(2)}, u32[]{:S(2)}) collective-permute-start(bf16[8,1536]{1,0:T(8,128)(2,1)} %get-tuple-element.17), channel_id=1, source_target_pairs={{0,2},{1,3},{2,0},{3,1},{4,6},{5,7},{6,4},{7,5},{8,10},{9,11},{10,... | collective-permute-start | bytes 73736 | tf_op jit(solution)/shard_map/ppermute | solution.py:22
  7.1 2.0 %collective-permute-done.3 = bf16[8,1536]{1,0:T(8,128)(2,1)S(1)} collective-permute-done((bf16[8,1536]{1,0:T(8,128)(2,1)}, bf16[8,1536]{1,0:T(8,128)(2,1)S(1)}, u32[]{:S(2)}, u32[]{:S(2)}) %collective-permute-start.3) | collective-permute-done | bytes 24608 | tf_op jit(solution)/shard_map/ppermute | solution.py:22
  9.1 0.7 %pad_maximum_fusion.3 = bf16[16,1536]{1,0:T(8,128)(2,1)S(1)} fusion(bf16[8,1536]{1,0:T(8,128)(2,1)S(1)} %collective-permute-done.3, bf16[8,1536]{1,0:T(8,128)(2,1)} %get-tuple-element.17), kind=kLoop, calls=%fused_computation.7 | loop fusion | flops 98304 | bytes 98304 | tf_op jit(solution)/shard_map/concatenate | solution.py:250
  9.8 3.0 %collective-permute-start.4 = (bf16[16,1536]{1,0:T(8,128)(2,1)S(1)}, bf16[16,1536]{1,0:T(8,128)(2,1)S(1)}, u32[]{:S(2)}, u32[]{:S(2)}) collective-permute-start(bf16[16,1536]{1,0:T(8,128)(2,1)S(1)} %pad_maximum_fusion.3), channel_id=1, source_target_pairs={{0,4},{1,5},{2,6},{3,7},{4,0},{5,1},{6,2},{7,3},{8,12},{9,13},{10,... | collective-permute-start | bytes 147464 | tf_op jit(solution)/shard_map/ppermute | solution.py:22
  12.9 1.5 %collective-permute-start = (bf16[128,1536]{1,0:T(8,128)(2,1)}, bf16[128,1536]{1,0:T(8,128)(2,1)S(1)}, u32[]{:S(2)}, u32[]{:S(2)}) collective-permute-start(bf16[128,1536]{1,0:T(8,128)(2,1)} %get-tuple-element.14), channel_id=1, source_target_pairs={{0,8},{8,0},{16,24},{24,16},{1,9},{9,1},{17,25},{25,17},{2,10},{10... | collective-permute-start | bytes 1179656 | tf_op jit(solution)/shard_map/ppermute | solution.py:22
  14.3 1.5 %collective-permute-start.2 = (bf16[128,1536]{1,0:T(8,128)(2,1)}, bf16[128,1536]{1,0:T(8,128)(2,1)S(1)}, u32[]{:S(2)}, u32[]{:S(2)}) collective-permute-start(bf16[128,1536]{1,0:T(8,128)(2,1)} %get-tuple-element.16), channel_id=1, source_target_pairs={{0,16},{8,24},{16,0},{24,8},{1,17},{9,25},{17,1},{25,9},{2,18},{10... | collective-permute-start | bytes 1179656 | tf_op jit(solution)/shard_map/ppermute | solution.py:22
  15.9 0.0 collective-permute-done.4
  15.9 0.9 %collective-permute-start.5 = (bf16[24,1536]{1,0:T(8,128)(2,1)S(1)}, bf16[24,1536]{1,0:T(8,128)(2,1)S(1)}, u32[]{:S(2)}, u32[]{:S(2)}) collective-permute-start(bf16[24,1536]{1,0:T(8,128)(2,1)S(1)} %pad_maximum_fusion.2), channel_id=1, source_target_pairs={{0,8},{8,0},{16,24},{24,16},{1,9},{9,1},{17,25},{25,17},{2,10},{10... | collective-permute-start | bytes 221192 | tf_op jit(solution)/shard_map/ppermute | solution.py:22
  16.7 0.9 %constant_dynamic-update-slice_fusion.3 = bf16[352,1536]{1,0:T(8,128)(2,1)S(1)} fusion(bf16[64,1536]{1,0:T(8,128)(2,1)} %get-tuple-element.18), kind=kLoop, calls=%fused_computation.11 | loop fusion | bytes 393216
  17.7 6.4 %collective-permute-done.5 = bf16[24,1536]{1,0:T(8,128)(2,1)S(1)} collective-permute-done((bf16[24,1536]{1,0:T(8,128)(2,1)S(1)}, bf16[24,1536]{1,0:T(8,128)(2,1)S(1)}, u32[]{:S(2)}, u32[]{:S(2)}) %collective-permute-start.5) | collective-permute-done | bytes 73760 | tf_op jit(solution)/shard_map/ppermute | solution.py:22
  24.1 0.0 collective-permute-done.refs_1_
  24.1 1.6 %collective-permute-start.6 = (bf16[176,1536]{1,0:T(8,128)(2,1)S(1)}, bf16[176,1536]{1,0:T(8,128)(2,1)S(1)}, u32[]{:S(2)}, u32[]{:S(2)}) collective-permute-start(bf16[176,1536]{1,0:T(8,128)(2,1)S(1)} %pad_maximum_fusion), channel_id=1, source_target_pairs={{0,16},{8,24},{16,0},{24,8},{1,17},{9,25},{17,1},{25,9},{2,18},{10... | collective-permute-start | bytes 1622024 | tf_op jit(solution)/shard_map/ppermute | solution.py:22
  25.7 0.0 collective-permute-done.2.refs_3_
  25.8 10.1 %collective-permute-done.6.refs_4_ = bf16[176,1536]{1,0:T(8,128)(2,1)S(1)} collective-permute-done((bf16[176,1536]{1,0:T(8,128)(2,1)S(1)}, bf16[176,1536]{1,0:T(8,128)(2,1)S(1)}, u32[]{:S(2)}, u32[]{:S(2)}) %collective-permute-start.6) | collective-permute-done | bytes 540704 | tf_op jit(solution)/shard_map/ppermute | solution.py:22
  35.9 0.1 collective-permute-start.7
  36.0 1.6 %collective-permute-start.1 = (bf16[128,1536]{1,0:T(8,128)(2,1)S(1)}, bf16[128,1536]{1,0:T(8,128)(2,1)S(1)}, u32[]{:S(2)}, u32[]{:S(2)}) collective-permute-start(bf16[128,1536]{1,0:T(8,128)(2,1)S(1)} %copy-done.4), channel_id=1, source_target_pairs={{0,8},{8,0},{16,24},{24,16},{1,9},{9,1},{17,25},{25,17},{2,10},{10... | collective-permute-start | bytes 1179656 | tf_op jit(solution)/shard_map/ppermute | solution.py:22
  37.6 7.3 %shard_map.56 = (f32[768,512]{1,0:T(8,128)}, f32[12,512]{1,0:T(8,128)}, f32[12,512]{1,0:T(8,128)}) custom-call(bf16[512,768]{1,0:T(8,128)(2,1)} %bitcast.6, bf16[512,1536]{1,0:T(8,128)(2,1)} %get-tuple-element.19.refs_1_), custom_call_target="tpu_custom_call" | custom-call | flops 3221225472 | bytes 3145728 | tf_op jit(solution)/shard_map/pallas_call | solution.py:209
  44.9 0.7 %pad_maximum_fusion.1.refs_6_ = bf16[48,1536]{1,0:T(8,128)(2,1)} fusion(bf16[24,1536]{1,0:T(8,128)(2,1)S(1)} %collective-permute-done.5, bf16[16,1536]{1,0:T(8,128)(2,1)S(1)} %collective-permute-done.4, bf16[8,1536]{1,0:T(8,128)(2,1)S(1)} %collective-permute-done.3), kind=kLoop, calls=%fused_computation.5 | loop fusion | flops 442368 | bytes 294912 | tf_op jit(solution)/shard_map/concatenate | solution.py:253
  45.6 2.0 %collective-permute-done.1.refs_2_ = bf16[128,1536]{1,0:T(8,128)(2,1)S(1)} collective-permute-done((bf16[128,1536]{1,0:T(8,128)(2,1)S(1)}, bf16[128,1536]{1,0:T(8,128)(2,1)S(1)}, u32[]{:S(2)}, u32[]{:S(2)}) %collective-permute-start.1) | collective-permute-done | bytes 393248 | tf_op jit(solution)/shard_map/ppermute | solution.py:22
  47.6 0.0 collective-permute-done.7.refs_5_
  47.6 0.8 %copy-done.5 = bf16[128,1536]{1,0:T(8,128)(2,1)} copy-done((bf16[128,1536]{1,0:T(8,128)(2,1)}, bf16[128,1536]{1,0:T(8,128)(2,1)S(1)}, u32[]{:S(2)}) %copy-start.5) | copy-done | bytes 393240
  48.3 0.4 copy-done.3
  48.7 12.3 %shard_map.57 = bf16[512,768]{1,0:T(8,128)(2,1)} custom-call(bf16[512,768]{1,0:T(8,128)(2,1)} %bitcast.7, bf16[128,1536]{1,0:T(8,128)(2,1)} %copy-done, bf16[128,1536]{1,0:T(8,128)(2,1)} %copy-done.5, bf16[128,1536]{1,0:T(8,128)(2,1)} %copy-done.2, bf16[176,1536]{1,0:T(8,128)(2,1)} %copy-done.1, bf16[352,1536]{1,0:T(8,128)(2,1)} %copy-done.3, ...), custom_call_target="tpu_custom_call" | custom-call | flops 6039797760 | bytes 4521984 | tf_op jit(solution)/shard_map/pallas_call | solution.py:209
  (19 shorter events, 0.1 us)
Async XLA Ops:
  4.0 5.0 %collective-permute-start.3 = (bf16[8,1536]{1,0:T(8,128)(2,1)}, bf16[8,1536]{1,0:T(8,128)(2,1)S(1)}, u32[]{:S(2)}, u32[]{:S(2)}) collective-permute-start(bf16[8,1536]{1,0:T(8,128)(2,1)} %get-tuple-element.17), channel_id=1, source_target_pairs={{0,2},{1,3},{2,0},{3,1},{4,6},{5,7},{6,4},{7,5},{8,10},{9,11},{10,... | collective-permute-start | bytes 73736 | tf_op jit(solution)/shard_map/ppermute | solution.py:22
  9.8 6.0 %collective-permute-start.4 = (bf16[16,1536]{1,0:T(8,128)(2,1)S(1)}, bf16[16,1536]{1,0:T(8,128)(2,1)S(1)}, u32[]{:S(2)}, u32[]{:S(2)}) collective-permute-start(bf16[16,1536]{1,0:T(8,128)(2,1)S(1)} %pad_maximum_fusion.3), channel_id=1, source_target_pairs={{0,4},{1,5},{2,6},{3,7},{4,0},{5,1},{6,2},{7,3},{8,12},{9,13},{10,... | collective-permute-start | bytes 147464 | tf_op jit(solution)/shard_map/ppermute | solution.py:22
  12.9 11.2 %collective-permute-start = (bf16[128,1536]{1,0:T(8,128)(2,1)}, bf16[128,1536]{1,0:T(8,128)(2,1)S(1)}, u32[]{:S(2)}, u32[]{:S(2)}) collective-permute-start(bf16[128,1536]{1,0:T(8,128)(2,1)} %get-tuple-element.14), channel_id=1, source_target_pairs={{0,8},{8,0},{16,24},{24,16},{1,9},{9,1},{17,25},{25,17},{2,10},{10... | collective-permute-start | bytes 1179656 | tf_op jit(solution)/shard_map/ppermute | solution.py:22
  14.3 11.4 %collective-permute-start.2 = (bf16[128,1536]{1,0:T(8,128)(2,1)}, bf16[128,1536]{1,0:T(8,128)(2,1)S(1)}, u32[]{:S(2)}, u32[]{:S(2)}) collective-permute-start(bf16[128,1536]{1,0:T(8,128)(2,1)} %get-tuple-element.16), channel_id=1, source_target_pairs={{0,16},{8,24},{16,0},{24,8},{1,17},{9,25},{17,1},{25,9},{2,18},{10... | collective-permute-start | bytes 1179656 | tf_op jit(solution)/shard_map/ppermute | solution.py:22
  15.9 8.2 %collective-permute-start.5 = (bf16[24,1536]{1,0:T(8,128)(2,1)S(1)}, bf16[24,1536]{1,0:T(8,128)(2,1)S(1)}, u32[]{:S(2)}, u32[]{:S(2)}) collective-permute-start(bf16[24,1536]{1,0:T(8,128)(2,1)S(1)} %pad_maximum_fusion.2), channel_id=1, source_target_pairs={{0,8},{8,0},{16,24},{24,16},{1,9},{9,1},{17,25},{25,17},{2,10},{10... | collective-permute-start | bytes 221192 | tf_op jit(solution)/shard_map/ppermute | solution.py:22
  24.1 11.8 %copy-start = (bf16[128,1536]{1,0:T(8,128)(2,1)}, bf16[128,1536]{1,0:T(8,128)(2,1)S(1)}, u32[]{:S(2)}) copy-start(bf16[128,1536]{1,0:T(8,128)(2,1)S(1)} %collective-permute-done.refs_1_) | copy-start | bytes 1179652
  24.1 11.9 %copy-start.4 = (bf16[128,1536]{1,0:T(8,128)(2,1)S(1)}, bf16[128,1536]{1,0:T(8,128)(2,1)}, u32[]{:S(2)}) copy-start(bf16[128,1536]{1,0:T(8,128)(2,1)} %get-tuple-element.15) | copy-start | bytes 1179652
  24.1 11.7 %collective-permute-start.6 = (bf16[176,1536]{1,0:T(8,128)(2,1)S(1)}, bf16[176,1536]{1,0:T(8,128)(2,1)S(1)}, u32[]{:S(2)}, u32[]{:S(2)}) collective-permute-start(bf16[176,1536]{1,0:T(8,128)(2,1)S(1)} %pad_maximum_fusion), channel_id=1, source_target_pairs={{0,16},{8,24},{16,0},{24,8},{1,17},{9,25},{17,1},{25,9},{2,18},{10... | collective-permute-start | bytes 1622024 | tf_op jit(solution)/shard_map/ppermute | solution.py:22
  25.7 19.1 %copy-start.2 = (bf16[128,1536]{1,0:T(8,128)(2,1)}, bf16[128,1536]{1,0:T(8,128)(2,1)S(1)}, u32[]{:S(2)}) copy-start(bf16[128,1536]{1,0:T(8,128)(2,1)S(1)} %collective-permute-done.2.refs_3_) | copy-start | bytes 1179652
  35.9 9.0 %copy-start.1 = (bf16[176,1536]{1,0:T(8,128)(2,1)}, bf16[176,1536]{1,0:T(8,128)(2,1)S(1)}, u32[]{:S(2)}) copy-start(bf16[176,1536]{1,0:T(8,128)(2,1)S(1)} %collective-permute-done.6.refs_4_) | copy-start | bytes 1622020
  35.9 11.6 %collective-permute-start.7 = (bf16[352,1536]{1,0:T(8,128)(2,1)S(1)}, bf16[352,1536]{1,0:T(8,128)(2,1)S(1)}, u32[]{:S(2)}, u32[]{:S(2)}) collective-permute-start(bf16[352,1536]{1,0:T(8,128)(2,1)S(1)} %slice_dynamic-update-slice_fusion.3), channel_id=1, source_target_pairs={{0,1},{1,0},{2,3},{3,2},{4,5},{5,4},{6,7},{7,6},{8,9},{9,8},{10,11... | collective-permute-start | bytes 3244040 | tf_op jit(solution)/shard_map/ppermute | solution.py:22
  36.0 11.5 %collective-permute-start.1 = (bf16[128,1536]{1,0:T(8,128)(2,1)S(1)}, bf16[128,1536]{1,0:T(8,128)(2,1)S(1)}, u32[]{:S(2)}, u32[]{:S(2)}) collective-permute-start(bf16[128,1536]{1,0:T(8,128)(2,1)S(1)} %copy-done.4), channel_id=1, source_target_pairs={{0,8},{8,0},{16,24},{24,16},{1,9},{9,1},{17,25},{25,17},{2,10},{10... | collective-permute-start | bytes 1179656 | tf_op jit(solution)/shard_map/ppermute | solution.py:22
  47.6 0.8 %copy-start.5 = (bf16[128,1536]{1,0:T(8,128)(2,1)}, bf16[128,1536]{1,0:T(8,128)(2,1)S(1)}, u32[]{:S(2)}) copy-start(bf16[128,1536]{1,0:T(8,128)(2,1)S(1)} %collective-permute-done.1.refs_2_) | copy-start | bytes 1179652
  47.6 1.1 %copy-start.3 = (bf16[352,1536]{1,0:T(8,128)(2,1)}, bf16[352,1536]{1,0:T(8,128)(2,1)S(1)}, u32[]{:S(2)}) copy-start(bf16[352,1536]{1,0:T(8,128)(2,1)S(1)} %collective-permute-done.7.refs_5_) | copy-start | bytes 3244036

commit v3 on v2

v3 whole, which is shorter than its diff:
```python
import math

import jax
import jax.numpy as jnp
import numpy as np
from jax import lax
from jax.experimental import pallas as pl
from jax.experimental.pallas import tpu as pltpu
from jax.sharding import PartitionSpec as P

HEAD_DIM = 64
GSTEP = 64
PAIR = 2 * HEAD_DIM
CHUNK = 256
COST = 1
LANES = 128
LOG2E = math.log2(math.e)
VMEM_BYTES = 24 * 1024 * 1024


def across(block, axis, bit):
    count = lax.axis_size(axis)
    return lax.ppermute(block, axis, [(i, i ^ (1 << bit)) for i in range(count)])


def after(block, *others):
    return lax.optimization_barrier((block, *others))[0]


def runs(counts):
    found = []
    for at, value in enumerate(counts):
        if found and found[-1][2] == value:
            found[-1][1] = at + 1
        else:
            found.append([at, at + 1, int(value)])
    return [tuple(entry) for entry in found]


def order_rows(select, key_rows, values, prefixes):
    tokens, width = key_rows.shape

    def kernel(select_ref, key_ref, value_ref, *out_refs):
        for half, ref in enumerate((key_ref, value_ref)):
            moved = jnp.dot(
                select_ref[...], ref[...], preferred_element_type=jnp.float32
            ).astype(jnp.bfloat16)
            for (low, high), out_ref in zip(prefixes, out_refs):
                out_ref[:, half * width : (half + 1) * width] = moved[low:high]

    return pl.pallas_call(
        kernel,
        out_shape=[
            jax.ShapeDtypeStruct((high - low, 2 * width), jnp.bfloat16) for low, high in prefixes
        ],
        compiler_params=pltpu.CompilerParams(vmem_limit_bytes=VMEM_BYTES),
        cost_estimate=pl.CostEstimate(
            flops=4 * select.size * width, bytes_accessed=6 * tokens * width, transcendentals=0
        ),
    )(select, key_rows, values)


def attend(queries, sets, counts=None, row_strides=None, part=(0, 1), states=(), out_weight=None, cost=1):
    tokens = queries.shape[0]
    width = queries.shape[1] // part[1]
    heads, pairs = width // HEAD_DIM, width // PAIR
    joined = [not isinstance(block, tuple) for block in sets]
    sizes = [(block if whole else block[0]).shape[0] for block, whole in zip(sets, joined)]
    keys = sum(sizes)
    padded = -(-keys // CHUNK) * CHUNK
    row_runs = [(0, keys, 1)] if counts is None else runs(counts)
    scale = HEAD_DIM**-0.5 * LOG2E
    final = out_weight is not None
    groups = max(len(states), 1)

    def kernel(*refs):
        refs = list(refs)
        query_ref = refs.pop(0)
        set_refs = []
        for whole in joined:
            ref = refs.pop(0)
            set_refs.append((ref, 0, ref, width) if whole else (ref, 0, refs.pop(0), 0))
        state_refs = [[refs.pop(0) for _ in range(3)] for _ in states]
        if final:
            weight_ref, out_ref, attended_ref = refs.pop(0), refs.pop(0), refs.pop(-1)
        else:
            numer_out, peak_out, total_out = [refs.pop(0) for _ in range(3)]
        score_ref, value_ref = refs.pop(0), refs.pop(0)
        if row_strides is not None:
            offset_ref = refs.pop(0)
            row = lax.broadcasted_iota(jnp.int32, (keys, LANES), 0)
            rank = sum((row & (s - 1) == 0).astype(jnp.int32) for s in row_strides)
            offsets = jnp.zeros((keys, LANES), jnp.float32)
            for times in range(1, len(row_strides) + 1):
                offsets = jnp.where(rank == times, math.log2(1 + times), offsets)
            offset_ref[...] = offsets

        ones = jnp.ones((16, padded), jnp.bfloat16)
        key_chunks = []
        at = 0
        for entry, size in zip(set_refs, sizes):
            for low in range(0, size, CHUNK):
                count = min(CHUNK, size - low)
                key_chunks.append((entry[0], low, count, at))
                at += count
        value_chunks = list(range(0, padded, CHUNK))

        def column(pair):
            return pl.multiple_of(pair * PAIR, PAIR)

        def head_queries(pair, half):
            turned = query_ref[:, pl.ds(column(pair), PAIR)].T
            row = lax.broadcasted_iota(jnp.int32, turned.shape, 0)
            own = (row < HEAD_DIM) if half == 0 else (row >= HEAD_DIM)
            return jnp.where(own, turned, jnp.zeros_like(turned))

        def score(pair, half, query_head, chunk, running):
            ref, low, count, at = chunk
            scores = jnp.dot(
                ref[low : low + count, pl.ds(column(pair), PAIR)],
                query_head,
                preferred_element_type=jnp.float32,
            )
            score_ref[half, at : at + count, :] = scores
            tallest = jnp.max(scores.reshape(count // 8, 8, tokens), axis=0)
            return tallest if running is None else jnp.maximum(running, tallest)

        def weigh(half, peak, weighted, low, gathered):
            high = min(low + CHUNK, keys)
            pieces = []
            for first, last, times in row_runs:
                first, last = max(first, low), min(last, high)
                if first < last:
                    offset = peak - math.log2(times)
                    power = score_ref[half, first:last, :] * scale - offset
                    if row_strides is not None:
                        extra = offset_ref[first:last, :]
                        power = power + jnp.concatenate([extra] * (tokens // LANES), axis=1)
                    pieces.append(jnp.exp2(power))
            if low + CHUNK > keys:
                pieces.append(jnp.zeros((low + CHUNK - keys, tokens), jnp.float32))
            probs = (pieces[0] if len(pieces) == 1 else jnp.concatenate(pieces, axis=0)).astype(
                jnp.bfloat16
            )
            product = jnp.dot(
                weighted[:, low : low + CHUNK], probs, preferred_element_type=jnp.float32
            )
            return product if gathered is None else gathered + product

        def one_group(first_pair, last_pair, earlier):
            def local_rows(pair, half):
                start = (pair - first_pair) * PAIR + half * HEAD_DIM
                return pl.ds(pl.multiple_of(start, HEAD_DIM), HEAD_DIM)

            def local_head(pair, half):
                return pl.ds(2 * (pair - first_pair) + half, 1)

            def finish(pair, half, gathered, peak, before):
                numer, total = gathered[:HEAD_DIM], gathered[HEAD_DIM : HEAD_DIM + 1]
                if earlier is not None:
                    factor = jnp.exp2(before - peak)
                    numer = numer + factor * earlier[0][local_rows(pair, half), :]
                    total = total + factor * earlier[2][local_head(pair, half), :]
                start = pl.multiple_of(column(pair) + half * HEAD_DIM, HEAD_DIM)
                rows = pl.ds(start, HEAD_DIM)
                if final:
                    attended_ref[rows, :] = (numer / total).astype(jnp.bfloat16)
                else:
                    head = pl.ds(2 * pair + half, 1)
                    numer_out[rows, :] = numer
                    peak_out[head, :] = peak
                    total_out[head, :] = total

            def overlap(pair, half, running, values_t, next_pair, next_half):
                peak = jnp.max(running, axis=0, keepdims=True) * scale
                before = None
                if earlier is not None:
                    before = earlier[1][local_head(pair, half), :]
                    peak = jnp.maximum(peak, before)
                weighted = jnp.concatenate(
                    [values_t[half * HEAD_DIM : (half + 1) * HEAD_DIM], ones], axis=0
                )
                query_head = head_queries(next_pair, next_half)
                next_running, gathered = None, None
                for step in range(max(len(key_chunks), len(value_chunks))):
                    if step < len(key_chunks):
                        next_running = score(
                            next_pair, next_half, query_head, key_chunks[step], next_running
                        )
                    if step < len(value_chunks):
                        gathered = weigh(half, peak, weighted, value_chunks[step], gathered)
                finish(pair, half, gathered, peak, before)
                return next_running

            def pair_step(pair, running):
                at = 0
                for (_, _, ref, shift), size in zip(set_refs, sizes):
                    value_ref[at : at + size, :] = ref[:, pl.ds(column(pair) + shift, PAIR)]
                    at += size
                if padded > keys:
                    value_ref[keys:, :] = jnp.zeros((padded - keys, PAIR), jnp.bfloat16)
                values_t = value_ref[...].T
                running = overlap(pair, 0, running, values_t, pair, 1)
                later = jnp.minimum(pair + 1, last_pair - 1)
                return overlap(pair, 1, running, values_t, later, 0)

            first_head = head_queries(first_pair, 0)
            running = None
            for chunk in key_chunks:
                running = score(first_pair, 0, first_head, chunk, running)
            lax.fori_loop(first_pair, last_pair, pair_step, running)

        for group in range(groups):
            one_group(
                group * pairs // groups,
                (group + 1) * pairs // groups,
                state_refs[group] if states else None,
            )
        if final:
            out_ref[...] = lax.dot_general(
                attended_ref[...],
                weight_ref[...],
                (((0,), (0,)), ((), ())),
                preferred_element_type=jnp.float32,
            ).astype(jnp.bfloat16)

    if final:
        out_shape = jax.ShapeDtypeStruct((tokens, width), jnp.bfloat16)
    else:
        out_shape = [
            jax.ShapeDtypeStruct((width, tokens), jnp.float32),
            jax.ShapeDtypeStruct((heads, tokens), jnp.float32),
            jax.ShapeDtypeStruct((heads, tokens), jnp.float32),
        ]
    scratch = [
        pltpu.VMEM((2, padded, tokens), jnp.float32),
        pltpu.VMEM((padded, PAIR), jnp.bfloat16),
    ]
    if row_strides is not None:
        scratch.append(pltpu.VMEM((keys, LANES), jnp.float32))
    if final:
        scratch.append(pltpu.VMEM((width, tokens), jnp.bfloat16))
    whole_spec = pl.BlockSpec(memory_space=pltpu.VMEM)

    def part_spec(block):
        if part[1] == 1:
            return whole_spec
        return pl.BlockSpec((block.shape[0], block.shape[1] // part[1]), lambda step: (0, part[0]))

    operands, specs = [queries], [part_spec(queries)]
    for block, whole in zip(sets, joined):
        for array in (block,) if whole else block:
            operands.append(array)
            specs.append(part_spec(array))
    for array in [array for state in states for array in state] + ([out_weight] if final else []):
        operands.append(array)
        specs.append(whole_spec)
    return pl.pallas_call(
        kernel,
        out_shape=out_shape,
        grid=(1,) if part[1] > 1 else (),
        in_specs=specs,
        scratch_shapes=scratch,
        compiler_params=pltpu.CompilerParams(vmem_limit_bytes=VMEM_BYTES),
        cost_estimate=pl.CostEstimate(
            flops=16 * tokens * keys * width // cost,
            bytes_accessed=(4 * keys * width + 4 * tokens * width) // cost,
            transcendentals=tokens * keys * heads // cost,
        ),
    )(*operands)


def local(queries, key_rows, values, out_weight):
    query_rows, own_keys, own_values = queries[0], key_rows[0], values[0]
    tokens = query_rows.shape[0]
    inner_bits = lax.axis_size("inner").bit_length() - 1
    outer_bits = lax.axis_size("outer").bit_length() - 1
    strides = [1 << (bit + 1) for bit in range(inner_bits + 1)] + [GSTEP]
    sends = [tokens >> (bit + 1) for bit in range(inner_bits + 1)]
    n_global = tokens // GSTEP

    rows = np.arange(0, tokens, 2)
    rank = sum((rows % s == 0).astype(np.int64) for s in strides)
    order = rows[np.lexsort((rows, -rank))]
    select = np.zeros((sends[0], tokens), np.float32)
    select[np.arange(sends[0]), order] = 1.0

    def prefix_counts(level, length):
        return sum((order[:length] % s == 0).astype(np.int64) for s in strides[level:])

    first_a, first_b, own_global = order_rows(
        jnp.asarray(select, jnp.bfloat16),
        own_keys,
        own_values,
        [(0, sends[1]), (sends[1], sends[0]), (0, n_global)],
    )

    far = own_global
    came = across(far, "outer", 1) if outer_bits > 1 else None
    near_a = across(first_a, "inner", 0)
    direct = [across(first_a[: sends[bit]], "inner", bit) for bit in range(1, inner_bits)]
    near_b = across(first_b, "inner", 0)
    own_set = [(own_keys, own_values)]
    state_a = attend(query_rows, own_set, row_strides=strides, part=(0, 2), cost=COST)
    for bit in range(1, outer_bits):
        if bit > 1:
            came = across(far, "outer", bit)
        far = jnp.concatenate([far, came], axis=0)
    far = far[n_global:]
    state_b = attend(
        after(query_rows, near_a), own_set, row_strides=strides, part=(1, 2), cost=COST
    )
    far = after(far, state_a[1])
    far = jnp.concatenate([far, across(far, "inner", 0)], axis=0)

    sets, counts = [near_a, near_b], [prefix_counts(0, sends[0])]
    held = [near_a]
    early = None
    for bit in range(1, inner_bits):
        count = sends[bit]
        moved = [block[:count] for block in held]
        moved = moved[0] if len(moved) == 1 else jnp.concatenate(moved, axis=0)
        if bit == 1:
            moved = after(moved, state_a[1])
        came = across(moved, "inner", bit)
        far = after(far, state_b[1])
        far = jnp.concatenate([far, across(far, "inner", bit)], axis=0)
        if early is None:
            counts.append(prefix_counts(bit, count))
            early = attend(
                query_rows,
                sets + [direct[0]],
                np.concatenate(counts),
                states=[state_a, state_b],
                cost=COST,
            )
            sets, counts = [came], [prefix_counts(bit, count)] * len(held)
        else:
            sets += [direct[bit - 1], came]
            counts += [prefix_counts(bit, count)] * (1 + len(held))
        held = held + [direct[bit - 1]]
        held += [came[at : at + count] for at in range(0, came.shape[0], count)]
    count = sends[inner_bits]
    moved = jnp.concatenate([block[:count] for block in [first_a] + held] + [far], axis=0)
    if early is not None:
        moved = after(moved, early[1])
    came = across(moved, "outer", 0)
    sets += [came, far]
    counts += [prefix_counts(inner_bits, count)] * (1 + len(held))
    counts.append(np.ones(2 * far.shape[0], np.int64))
    states = [early] if early is not None else [state_a, state_b]
    result = attend(
        query_rows, sets, np.concatenate(counts), states=states, out_weight=out_weight
    )
    return result[None]


def solution(mesh):
    placed = (P("outer", "inner", None), P("outer", "inner", None), P("outer", "inner", None), P())
    return jax.shard_map(
        local, mesh=mesh, in_specs=placed, out_specs=P("outer", "inner", None), check_vma=False
    )
```

time: 61.2 us -> 53.7 us (0.88)
  Pallas kernels: 23.6 us -> 18.7 us
  waiting for transfers between devices: 20.5 us -> 17.1 us
  local copies, waits for them, and re-layouts: 2.14 us -> 4.44 us
  other arithmetic: 1.47 us -> 0.04 us
    pallas_call x3 -> x5, Pallas kernels: 23.6 us -> 18.7 us  [the longest x4 18.1 us: attend(): pl.pallas_call(kernel, out_shape=out_shape, grid=(1,) if part[1] > 1 else...]
    ppermute x8 -> x9, waiting for transfers between devices: 20.5 us -> 17.1 us  [across(): return lax.ppermute(block, axis, [(i, i ^ 1 << bit) for i in range(count)])]
    unnamed x19, local copies, waits for them, and re-layouts: 2.13 us -> 4.43 us
    concatenate x2, other arithmetic: 0.75 us -> 0.01 us  [local(): far = jnp.concatenate([far, came], axis=0)]
    concatenate x1, other arithmetic: 0.68 us -> 0.01 us  [local(): far = jnp.concatenate([far, across(far, 'inner', 0)], axis=0)]
    ppermute x8 -> x9, starting transfers between devices: 13.2 us -> 13 us  [across(): return lax.ppermute(block, axis, [(i, i ^ 1 << bit) for i in range(count)])]
  transfers between devices with their start and end apart: 8 -> 9, of which waited for: 4 -> 3; matrix products, arithmetic and copies ran while one was open for 3% -> 0% of each run, Pallas kernels for 12% -> 20%
where the time goes in v3:
time: 53.7 us; the launch traced here: 53.5 us
  Pallas kernels  18.7 us (35%)
  waiting for transfers between devices  17.1 us (32%)
  starting transfers between devices  13 us (24%)
  local copies, waits for them, and re-layouts  4.44 us (8%)
    pallas_call x4, Pallas kernels, attend(): pl.pallas_call(kernel, out_shape=out_shape, grid=(1,) if part[1] > 1 else...  18.1 us
    ppermute x9, waiting for transfers between devices, across(): return lax.ppermute(block, axis, [(i, i ^ 1 << bit) for i in range(count)])  17.1 us
    ppermute x9, starting transfers between devices, across(): return lax.ppermute(block, axis, [(i, i ^ 1 << bit) for i in range(count)])  13 us
    unnamed x19, local copies, waits for them, and re-layouts  4.43 us
  transfers between devices with their start and end apart: 9, of which 3 were waited for; matrix products, arithmetic and copies ran while one was open for 0% of the time, Pallas kernels for 20%

profile of v3, /device:TPU:0, one launch (start us, length us, event | category | flops | bytes accessed | tf_op | source)
XLA Modules:
  0.0 53.5 jit_solution(4464735161353629561)
XLA Ops:
  0.0 1.1 %copy-done = bf16[1,512,768]{2,1,0:T(8,128)(2,1)S(1)} copy-done((bf16[1,512,768]{2,1,0:T(8,128)(2,1)S(1)}, bf16[1,512,768]{2,1,0:T(8,128)(2,1)}, u32[]{:S(2)}) %copy-start) | copy-done | bytes 786456
  1.1 1.1 %copy-done.2 = bf16[1,512,768]{2,1,0:T(8,128)(2,1)S(1)} copy-done((bf16[1,512,768]{2,1,0:T(8,128)(2,1)S(1)}, bf16[1,512,768]{2,1,0:T(8,128)(2,1)}, u32[]{:S(2)}) %copy-start.2) | copy-done | bytes 786456
  2.3 0.9 %copy-done.4 = bf16[256,512]{1,0:T(8,128)(2,1)S(1)} copy-done((bf16[256,512]{1,0:T(8,128)(2,1)S(1)}, bf16[256,512]{1,0:T(8,128)(2,1)}, u32[]{:S(2)}) %copy-start.4) | copy-done | bytes 262168
  3.2 0.6 %shard_map.55 = (bf16[128,1536]{1,0:T(8,128)(2,1)S(1)}, bf16[128,1536]{1,0:T(8,128)(2,1)S(1)}, bf16[8,1536]{1,0:T(8,128)(2,1)S(1)}) custom-call(bf16[256,512]{1,0:T(8,128)(2,1)S(1)} %copy-done.4, bf16[512,768]{1,0:T(8,128)(2,1)S(1)} %bitcast.4, bf16[512,768]{1,0:T(8,128)(2,1)S(1)} %bitcast.7), custom_call_target="tpu_custom_call" | custom-call | flops 402653184 | bytes 2359296 | tf_op jit(solution)/shard_map/pallas_call | solution.py:51
  3.8 3.1 %collective-permute-start.3 = (bf16[8,1536]{1,0:T(8,128)(2,1)S(1)}, bf16[8,1536]{1,0:T(8,128)(2,1)S(1)}, u32[]{:S(2)}, u32[]{:S(2)}) collective-permute-start(bf16[8,1536]{1,0:T(8,128)(2,1)S(1)} %get-tuple-element.25), channel_id=1, source_target_pairs={{0,2},{1,3},{2,0},{3,1},{4,6},{5,7},{6,4},{7,5},{8,10},{9,11},{10,... | collective-permute-start | bytes 73736 | tf_op jit(solution)/shard_map/ppermute | solution.py:23
  6.9 1.5 %collective-permute-start = (bf16[128,1536]{1,0:T(8,128)(2,1)S(1)}, bf16[128,1536]{1,0:T(8,128)(2,1)S(1)}, u32[]{:S(2)}, u32[]{:S(2)}) collective-permute-start(bf16[128,1536]{1,0:T(8,128)(2,1)S(1)} %get-tuple-element.22), channel_id=1, source_target_pairs={{0,8},{8,0},{16,24},{24,16},{1,9},{9,1},{17,25},{25,17},{2,10},{10... | collective-permute-start | bytes 1179656 | tf_op jit(solution)/shard_map/ppermute | solution.py:23
  8.4 1.5 %collective-permute-start.2 = (bf16[128,1536]{1,0:T(8,128)(2,1)S(1)}, bf16[128,1536]{1,0:T(8,128)(2,1)S(1)}, u32[]{:S(2)}, u32[]{:S(2)}) collective-permute-start(bf16[128,1536]{1,0:T(8,128)(2,1)S(1)} %get-tuple-element.22), channel_id=1, source_target_pairs={{0,16},{8,24},{16,0},{24,8},{1,17},{9,25},{17,1},{25,9},{2,18},{10... | collective-permute-start | bytes 1179656 | tf_op jit(solution)/shard_map/ppermute | solution.py:23
  9.9 0.5 %collective-permute-start.7 = (bf16[128,1536]{1,0:T(8,128)(2,1)S(1)}, bf16[128,1536]{1,0:T(8,128)(2,1)S(1)}, u32[]{:S(2)}, u32[]{:S(2)}) collective-permute-start(bf16[128,1536]{1,0:T(8,128)(2,1)S(1)} %get-tuple-element.30), channel_id=1, source_target_pairs={{0,8},{8,0},{16,24},{24,16},{1,9},{9,1},{17,25},{25,17},{2,10},{10... | collective-permute-start | bytes 1179656 | tf_op jit(solution)/shard_map/ppermute | solution.py:23
  10.4 0.0 collective-permute-done.3
  10.4 2.6 %collective-permute-start.4 = (bf16[16,1536]{1,0:T(8,128)(2,1)S(1)}, bf16[16,1536]{1,0:T(8,128)(2,1)S(1)}, u32[]{:S(2)}, u32[]{:S(2)}) collective-permute-start(bf16[16,1536]{1,0:T(8,128)(2,1)S(1)} %pad_maximum_fusion.3), channel_id=1, source_target_pairs={{0,4},{1,5},{2,6},{3,7},{4,0},{5,1},{6,2},{7,3},{8,12},{9,13},{10,... | collective-permute-start | bytes 147464 | tf_op jit(solution)/shard_map/ppermute | solution.py:23
  13.1 1.1 %copy-done.6 = bf16[1,512,768]{2,1,0:T(8,128)(2,1)S(1)} copy-done((bf16[1,512,768]{2,1,0:T(8,128)(2,1)S(1)}, bf16[1,512,768]{2,1,0:T(8,128)(2,1)}, u32[]{:S(2)}) %copy-start.6) | copy-done | bytes 786456
  14.2 3.0 %shard_map.56 = (f32[384,512]{1,0:T(8,128)S(1)}, f32[6,512]{1,0:T(8,128)S(1)}, f32[6,512]{1,0:T(8,128)S(1)}) custom-call(bf16[512,768]{1,0:T(8,128)(2,1)S(1)} %bitcast.10, bf16[512,768]{1,0:T(8,128)(2,1)S(1)} %bitcast.5, bf16[512,768]{1,0:T(8,128)(2,1)S(1)} %bitcast.8), custom_call_target="tpu_custom_call" | custom-call | flops 1610612736 | bytes 1572864 | tf_op jit(solution)/shard_map/pallas_call | solution.py:258
  17.3 1.6 %collective-permute-start.5 = (bf16[24,1536]{1,0:T(8,128)(2,1)S(1)}, bf16[24,1536]{1,0:T(8,128)(2,1)S(1)}, u32[]{:S(2)}, u32[]{:S(2)}) collective-permute-start(bf16[24,1536]{1,0:T(8,128)(2,1)S(1)} %pad_maximum_fusion.2), channel_id=1, source_target_pairs={{0,8},{8,0},{16,24},{24,16},{1,9},{9,1},{17,25},{25,17},{2,10},{10... | collective-permute-start | bytes 221192 | tf_op jit(solution)/shard_map/ppermute | solution.py:23
  18.8 8.6 %collective-permute-done.5 = bf16[24,1536]{1,0:T(8,128)(2,1)S(1)} collective-permute-done((bf16[24,1536]{1,0:T(8,128)(2,1)S(1)}, bf16[24,1536]{1,0:T(8,128)(2,1)S(1)}, u32[]{:S(2)}, u32[]{:S(2)}) %collective-permute-start.5) | collective-permute-done | bytes 73760 | tf_op jit(solution)/shard_map/ppermute | solution.py:23
  27.5 3.0 %shard_map.57 = (f32[384,512]{1,0:T(8,128)S(1)}, f32[6,512]{1,0:T(8,128)S(1)}, f32[6,512]{1,0:T(8,128)S(1)}) custom-call(bf16[512,768]{1,0:T(8,128)(2,1)S(1)} %bitcast.11, bf16[512,768]{1,0:T(8,128)(2,1)S(1)} %bitcast.6, bf16[512,768]{1,0:T(8,128)(2,1)S(1)} %bitcast.9), custom_call_target="tpu_custom_call" | custom-call | flops 1610612736 | bytes 1572864 | tf_op jit(solution)/shard_map/pallas_call | solution.py:258
  30.5 1.6 %collective-permute-start.6 = (bf16[48,1536]{1,0:T(8,128)(2,1)S(1)}, bf16[48,1536]{1,0:T(8,128)(2,1)S(1)}, u32[]{:S(2)}, u32[]{:S(2)}) collective-permute-start(bf16[48,1536]{1,0:T(8,128)(2,1)S(1)} %pad_maximum_fusion.1), channel_id=1, source_target_pairs={{0,16},{8,24},{16,0},{24,8},{1,17},{9,25},{17,1},{25,9},{2,18},{10... | collective-permute-start | bytes 442376 | tf_op jit(solution)/shard_map/ppermute | solution.py:23
  32.1 0.5 collective-permute-start.1
  32.6 0.0 collective-permute-done.2.refs_3_
  32.6 4.9 %shard_map.58 = (f32[768,512]{1,0:T(8,128)S(1)}, f32[12,512]{1,0:T(8,128)S(1)}, f32[12,512]{1,0:T(8,128)S(1)}) custom-call(bf16[512,768]{1,0:T(8,128)(2,1)S(1)} %bitcast.12, bf16[128,1536]{1,0:T(8,128)(2,1)S(1)} %collective-permute-done.refs_1_, bf16[128,1536]{1,0:T(8,128)(2,1)S(1)} %collective-permute-done.7.refs_2_, ...), custom_call_target="tpu_custom_call" | custom-call | flops 2415919104 | bytes 2752512 | tf_op jit(solution)/shard_map/pallas_call | solution.py:258
  37.5 0.0 copy-start.5
  37.6 5.8 %collective-permute-done.1.refs_1_ = bf16[128,1536]{1,0:T(8,128)(2,1)S(1)} collective-permute-done((bf16[128,1536]{1,0:T(8,128)(2,1)S(1)}, bf16[128,1536]{1,0:T(8,128)(2,1)S(1)}, u32[]{:S(2)}, u32[]{:S(2)}) %collective-permute-start.1) | collective-permute-done | bytes 393248 | tf_op jit(solution)/shard_map/ppermute | solution.py:23
  43.5 0.1 collective-permute-start.8
  43.6 2.7 %collective-permute-done.8.refs_2_ = bf16[352,1536]{1,0:T(8,128)(2,1)S(1)} collective-permute-done((bf16[352,1536]{1,0:T(8,128)(2,1)S(1)}, bf16[352,1536]{1,0:T(8,128)(2,1)S(1)}, u32[]{:S(2)}, u32[]{:S(2)}) %collective-permute-start.8) | collective-permute-done | bytes 1081376 | tf_op jit(solution)/shard_map/ppermute | solution.py:23
  46.2 7.2 %shard_map.59 = bf16[512,768]{1,0:T(8,128)(2,1)} custom-call(bf16[512,768]{1,0:T(8,128)(2,1)S(1)} %bitcast.13, bf16[128,1536]{1,0:T(8,128)(2,1)S(1)} %collective-permute-done.1.refs_1_, bf16[352,1536]{1,0:T(8,128)(2,1)S(1)} %collective-permute-done.8.refs_2_, bf16[96,1536]{1,0:T(8,128)(2,1)S(1)} %pad_maximum_fusion.refs_3_, ...), custom_call_target="tpu_custom_call" | custom-call | flops 3623878656 | bytes 3342336 | tf_op jit(solution)/shard_map/pallas_call | solution.py:258
  (23 shorter events, 0.2 us)
Async XLA Ops:
  0.0 1.1 %copy-start = (bf16[1,512,768]{2,1,0:T(8,128)(2,1)S(1)}, bf16[1,512,768]{2,1,0:T(8,128)(2,1)}, u32[]{:S(2)}) copy-start(bf16[1,512,768]{2,1,0:T(8,128)(2,1)} %param.6) | copy-start | bytes 2359300
  1.1 1.1 %copy-start.2 = (bf16[1,512,768]{2,1,0:T(8,128)(2,1)S(1)}, bf16[1,512,768]{2,1,0:T(8,128)(2,1)}, u32[]{:S(2)}) copy-start(bf16[1,512,768]{2,1,0:T(8,128)(2,1)} %param.7) | copy-start | bytes 2359300
  2.3 0.9 %copy-start.4 = (bf16[256,512]{1,0:T(8,128)(2,1)S(1)}, bf16[256,512]{1,0:T(8,128)(2,1)}, u32[]{:S(2)}) copy-start(bf16[256,512]{1,0:T(8,128)(2,1)} %constant.2.clone.select_ref) | copy-start | bytes 786436
  3.2 9.9 %copy-start.1 = (bf16[1,512,768]{2,1,0:T(8,128)(2,1)S(1)}, bf16[1,512,768]{2,1,0:T(8,128)(2,1)}, u32[]{:S(2)}) copy-start(bf16[1,512,768]{2,1,0:T(8,128)(2,1)} %param.6) | copy-start | bytes 2359300
  3.2 9.9 %copy-start.3 = (bf16[1,512,768]{2,1,0:T(8,128)(2,1)S(1)}, bf16[1,512,768]{2,1,0:T(8,128)(2,1)}, u32[]{:S(2)}) copy-start(bf16[1,512,768]{2,1,0:T(8,128)(2,1)} %param.7) | copy-start | bytes 2359300
  3.8 6.6 %collective-permute-start.3 = (bf16[8,1536]{1,0:T(8,128)(2,1)S(1)}, bf16[8,1536]{1,0:T(8,128)(2,1)S(1)}, u32[]{:S(2)}, u32[]{:S(2)}) collective-permute-start(bf16[8,1536]{1,0:T(8,128)(2,1)S(1)} %get-tuple-element.25), channel_id=1, source_target_pairs={{0,2},{1,3},{2,0},{3,1},{4,6},{5,7},{6,4},{7,5},{8,10},{9,11},{10,... | collective-permute-start | bytes 73736 | tf_op jit(solution)/shard_map/ppermute | solution.py:23
  6.9 20.6 %collective-permute-start = (bf16[128,1536]{1,0:T(8,128)(2,1)S(1)}, bf16[128,1536]{1,0:T(8,128)(2,1)S(1)}, u32[]{:S(2)}, u32[]{:S(2)}) collective-permute-start(bf16[128,1536]{1,0:T(8,128)(2,1)S(1)} %get-tuple-element.22), channel_id=1, source_target_pairs={{0,8},{8,0},{16,24},{24,16},{1,9},{9,1},{17,25},{25,17},{2,10},{10... | collective-permute-start | bytes 1179656 | tf_op jit(solution)/shard_map/ppermute | solution.py:23
  8.4 24.2 %collective-permute-start.2 = (bf16[128,1536]{1,0:T(8,128)(2,1)S(1)}, bf16[128,1536]{1,0:T(8,128)(2,1)S(1)}, u32[]{:S(2)}, u32[]{:S(2)}) collective-permute-start(bf16[128,1536]{1,0:T(8,128)(2,1)S(1)} %get-tuple-element.22), channel_id=1, source_target_pairs={{0,16},{8,24},{16,0},{24,8},{1,17},{9,25},{17,1},{25,9},{2,18},{10... | collective-permute-start | bytes 1179656 | tf_op jit(solution)/shard_map/ppermute | solution.py:23
  9.9 22.7 %collective-permute-start.7 = (bf16[128,1536]{1,0:T(8,128)(2,1)S(1)}, bf16[128,1536]{1,0:T(8,128)(2,1)S(1)}, u32[]{:S(2)}, u32[]{:S(2)}) collective-permute-start(bf16[128,1536]{1,0:T(8,128)(2,1)S(1)} %get-tuple-element.30), channel_id=1, source_target_pairs={{0,8},{8,0},{16,24},{24,16},{1,9},{9,1},{17,25},{25,17},{2,10},{10... | collective-permute-start | bytes 1179656 | tf_op jit(solution)/shard_map/ppermute | solution.py:23
  10.4 6.8 %collective-permute-start.4 = (bf16[16,1536]{1,0:T(8,128)(2,1)S(1)}, bf16[16,1536]{1,0:T(8,128)(2,1)S(1)}, u32[]{:S(2)}, u32[]{:S(2)}) collective-permute-start(bf16[16,1536]{1,0:T(8,128)(2,1)S(1)} %pad_maximum_fusion.3), channel_id=1, source_target_pairs={{0,4},{1,5},{2,6},{3,7},{4,0},{5,1},{6,2},{7,3},{8,12},{9,13},{10,... | collective-permute-start | bytes 147464 | tf_op jit(solution)/shard_map/ppermute | solution.py:23
  13.1 1.1 %copy-start.6 = (bf16[1,512,768]{2,1,0:T(8,128)(2,1)S(1)}, bf16[1,512,768]{2,1,0:T(8,128)(2,1)}, u32[]{:S(2)}) copy-start(bf16[1,512,768]{2,1,0:T(8,128)(2,1)} %param.5) | copy-start | bytes 2359300
  17.3 10.2 %collective-permute-start.5 = (bf16[24,1536]{1,0:T(8,128)(2,1)S(1)}, bf16[24,1536]{1,0:T(8,128)(2,1)S(1)}, u32[]{:S(2)}, u32[]{:S(2)}) collective-permute-start(bf16[24,1536]{1,0:T(8,128)(2,1)S(1)} %pad_maximum_fusion.2), channel_id=1, source_target_pairs={{0,8},{8,0},{16,24},{24,16},{1,9},{9,1},{17,25},{25,17},{2,10},{10... | collective-permute-start | bytes 221192 | tf_op jit(solution)/shard_map/ppermute | solution.py:23
  30.5 12.9 %collective-permute-start.6 = (bf16[48,1536]{1,0:T(8,128)(2,1)S(1)}, bf16[48,1536]{1,0:T(8,128)(2,1)S(1)}, u32[]{:S(2)}, u32[]{:S(2)}) collective-permute-start(bf16[48,1536]{1,0:T(8,128)(2,1)S(1)} %pad_maximum_fusion.1), channel_id=1, source_target_pairs={{0,16},{8,24},{16,0},{24,8},{1,17},{9,25},{17,1},{25,9},{2,18},{10... | collective-permute-start | bytes 442376 | tf_op jit(solution)/shard_map/ppermute | solution.py:23
  32.1 11.3 %collective-permute-start.1 = (bf16[128,1536]{1,0:T(8,128)(2,1)S(1)}, bf16[128,1536]{1,0:T(8,128)(2,1)S(1)}, u32[]{:S(2)}, u32[]{:S(2)}) collective-permute-start(bf16[128,1536]{1,0:T(8,128)(2,1)S(1)} %collective-permute-done.refs_1_), channel_id=1, source_target_pairs={{0,16},{8,24},{16,0},{24,8},{1,17},{9,25},{17,1},{25,9},{2,18},{10... | collective-permute-start | bytes 1179656 | tf_op jit(solution)/shard_map/ppermute | solution.py:23
  37.5 8.7 %copy-start.5 = (bf16[768,768]{1,0:T(8,128)(2,1)S(1)}, bf16[768,768]{1,0:T(8,128)(2,1)}, u32[]{:S(2)}) copy-start(bf16[768,768]{1,0:T(8,128)(2,1)} %refs_7_.1) | copy-start | bytes 3538948
  43.5 2.8 %collective-permute-start.8 = (bf16[352,1536]{1,0:T(8,128)(2,1)S(1)}, bf16[352,1536]{1,0:T(8,128)(2,1)S(1)}, u32[]{:S(2)}, u32[]{:S(2)}) collective-permute-start(bf16[352,1536]{1,0:T(8,128)(2,1)S(1)} %constant_dynamic-update-slice_fusion), channel_id=1, source_target_pairs={{0,1},{1,0},{2,3},{3,2},{4,5},{5,4},{6,7},{7,6},{8,9},{9,8},{10,11... | collective-permute-start | bytes 3244040 | tf_op jit(solution)/shard_map/ppermute | solution.py:23
